TPU v7x, 32 devices: a whole 2x2x4 slice. The times are simulated.
32 devices in a mesh: seq: 8 (over y, x, core), mp: 4 (over z).
Axes of the slice: x: 2, y: 2, z: 4, core: 2. Of those that a mesh axis runs over, the one named last changes fastest.
Arguments:
- stream: float32 [8, 1024, 2048], P(None, 'seq'), may hold values from -6 to 6
- norm_in: float32 [2048], replicated, may hold values from 0.5 to 1.5
- w_branch: bfloat16 [2048, 2560], P(None, 'mp'), may hold values from -0.125 to 0.125
- w_input: bfloat16 [2048, 2560], P(None, 'mp'), may hold values from -0.125 to 0.125
- conv_kernel: float32 [4, 2560], P(None, 'mp'), may hold values from -3 to 3
- conv_bias: float32 [2560], P('mp'), may hold values from -3 to 3
- gate_r: bfloat16 [16, 160, 160], P('mp'), may hold values from -0.5 to 0.5
- bias_r: float32 [2560], P('mp'), may hold values from -3 to 3
- gate_i: bfloat16 [16, 160, 160], P('mp'), may hold values from -0.5 to 0.5
- bias_i: float32 [2560], P('mp'), may hold values from -3 to 3
- decay_param: float32 [2560], P('mp'), may hold values from 4.5 to 9.3
- w_out: bfloat16 [2560, 2048], P('mp'), may hold values from -0.15625 to 0.15625
- norm_mlp: float32 [2048], replicated, may hold values from 0.5 to 1.5
- w_gate: bfloat16 [2048, 6144], P(None, 'mp'), may hold values from -0.125 to 0.125
- w_up: bfloat16 [2048, 6144], P(None, 'mp'), may hold values from -0.125 to 0.125
- w_down: bfloat16 [6144, 2048], P('mp'), may hold values from -0.15625 to 0.15625
- state_init: float32 [8, 2560], P(None, 'mp'), may hold values from -6 to 6
- conv_init: float32 [8, 3, 2560], P(None, None, 'mp'), may hold values from -6 to 6
- fresh_rows: int32 [8], replicated, may hold values from 0 to 1, as said below
- out_grad: float32 [8, 1024, 2048], P(None, 'seq'), may hold values from -8 to 8
Outputs:
- block_out: float32 [8, 1024, 2048], P(None, 'seq')
- stream_grad: float32 [8, 1024, 2048], P(None, 'seq')
- norm_in_grad: float32 [2048], replicated
- w_branch_grad: float32 [2048, 2560], P('seq', 'mp')
- w_input_grad: float32 [2048, 2560], P('seq', 'mp')
- conv_kernel_grad: float32 [4, 2560], P(None, 'mp')
- conv_bias_grad: float32 [2560], P('mp')
- gate_r_grad: float32 [16, 160, 160], P('mp')
- bias_r_grad: float32 [2560], P('mp')
- gate_i_grad: float32 [16, 160, 160], P('mp')
- bias_i_grad: float32 [2560], P('mp')
- decay_grad: float32 [2560], P('mp')
- w_out_grad: float32 [2560, 2048], P('mp', 'seq')
- norm_mlp_grad: float32 [2048], replicated
- w_gate_grad: float32 [2048, 6144], P('seq', 'mp')
- w_up_grad: float32 [2048, 6144], P('seq', 'mp')
- w_down_grad: float32 [6144, 2048], P('mp', 'seq')
- final_state: float32 [8, 2560], P(None, 'mp')
- final_conv: float32 [8, 3, 2560], P(None, None, 'mp')
Inputs may be any that keep to these rules, and one draw needn't show every extreme that they name: `fresh_rows`: half of the 8 sequences, chosen by the seed, are fresh.
All inputs are finite; a program needn't handle non-finite values.
Results may differ from a plain program's by a relative error of at most 0.0087.
Values sent between devices are 32-bit elements; how exact they have to be, the bound alone decides.
A program may use at most 320 MiB of HBM per device.

v0:
```python
import functools

import jax
import jax.numpy as jnp
from jax import lax
from jax.experimental import pallas as pl
from jax.experimental.pallas import tpu as pltpu
from jax.sharding import PartitionSpec as P

MESH = pl.DeviceIdType.MESH
RATE_SCALE = 8.0
EPS = 1e-06
GELU_C = 0.7978845608028654
GELU_K = 0.044715
CONTRACT_ROWS = (((0,), (0,)), ((), ()))
CONTRACT_LAST = (((1,), (1,)), ((), ()))
TILE = 8
LANES = 128
ROWS = 32
CHUNK = 16
SKEW = 2
GROUP = 16
WEIGHT_STEPS = 8
COPIES = 8
LATER = 6
F32 = jnp.float32
BF16 = jnp.bfloat16
VMEM = pl.BlockSpec(memory_space=pltpu.VMEM)
HBM = pl.BlockSpec(memory_space=pl.ANY)
PINNED = pl.BlockSpec(memory_space=pltpu.HBM)


def dot(a, b):
    return jnp.dot(a, b, preferred_element_type=F32)


def matmul_back(a, b):
    return lax.dot_general(a, b, CONTRACT_LAST, preferred_element_type=F32)


def block(i, size):
    return pl.ds(pl.multiple_of(i * size, size), size)


def gelu(x):
    t = jnp.tanh(GELU_C * (x + GELU_K * (x * x * x)))
    return 0.5 * x * (1.0 + t)


def gelu_both(x):
    x2 = x * x
    t = jnp.tanh(GELU_C * (x + GELU_K * (x2 * x)))
    half = 0.5 * (1.0 + t)
    slope = half + 0.5 * x * (1.0 - t * t) * (GELU_C * (1.0 + (3.0 * GELU_K) * x2))
    return x * half, slope


def one_minus_square(log_a, a):
    y = 2.0 * log_a
    s = 1.0 + y * (1.0 / 8.0)
    for k in (7, 6, 5, 4, 3, 2):
        s = 1.0 + (y * (1.0 / k)) * s
    return jnp.where(y > -0.35, -y * s, 1.0 - a * a)


def get(ref, at):
    return jnp.concatenate([ref[j, at, :] for j in range(ref.shape[0])], axis=-1)


def put(ref, at, value):
    for j in range(ref.shape[0]):
        ref[j, at, :] = value[:, j * LANES : (j + 1) * LANES]


def to_all(axis, src, slots, send, recv):
    size, me = lax.axis_size(axis), lax.axis_index(axis)
    return [
        pltpu.make_async_remote_copy(
            src_ref=src,
            dst_ref=slots.at[me],
            send_sem=send.at[d - 1],
            recv_sem=recv.at[d - 1],
            device_id={axis: lax.rem(me + d, size)},
            device_id_type=MESH,
        )
        for d in range(1, size)
    ]


def to_one(axis, distance, src, dst, send, recv):
    size, me = lax.axis_size(axis), lax.axis_index(axis)
    return pltpu.make_async_remote_copy(
        src_ref=src,
        dst_ref=dst,
        send_sem=send,
        recv_sem=recv,
        device_id={axis: lax.rem(me + distance + size, size)},
        device_id_type=MESH,
    )


def spread_gates(blocks_ref, out_ref, start, width):
    heads, size = blocks_ref.shape[:2]
    for h in range(heads):
        block_h = blocks_ref[h].astype(F32)
        parts = [block_h]
        if h > 0:
            parts.insert(0, jnp.zeros((size, h * size), F32))
        if width > (h + 1) * size:
            parts.append(jnp.zeros((size, width - (h + 1) * size), F32))
        row = jnp.concatenate(parts, axis=1).astype(BF16)
        out_ref[h * size : (h + 1) * size, start : start + width] = row
    if width > heads * size:
        rest = jnp.zeros((width - heads * size, width), BF16)
        out_ref[heads * size : width, start : start + width] = rest


def forward_kernel(
    span,
    x_in,
    w_input_in,
    w_branch_in,
    gain_ref,
    taps_ref,
    conv_bias_ref,
    decay_ref,
    bias_r_ref,
    bias_i_ref,
    gate_r_ref,
    gate_i_ref,
    fresh_ref,
    state_ref,
    conv_init_ref,
    normed_out,
    branch_out,
    pad_out,
    pre_out,
    hidden_out,
    mixed_ref,
    carry_ref,
    sums_ref,
    gates_ref,
    vec_ref,
    ends_ref,
    x_ref,
    w_input_ref,
    w_branch_ref,
    normed_ref,
    branch_ref,
    pad_ref,
    pre_ref,
    hidden_ref,
    act_ref,
    a_ref,
    b_ref,
    conv_ref,
    tail_ref,
    tail_in,
    mine_ref,
    load_sem,
    store_sem,
    normed_sem,
    send1,
    recv1,
    send_t,
    recv_t,
):
    seqs = state_ref.shape[0]
    width = taps_ref.shape[1]
    taps = taps_ref.shape[0]
    rows = seqs * span
    devices, me = lax.axis_size("seq"), lax.axis_index("seq")
    local = pltpu.make_async_copy
    pitch = a_ref.shape[1] // seqs
    group = 2 * span
    groups = rows // group

    def x_load(g):
        at = block(g, group)
        return local(x_in.at[at], x_ref.at[at], load_sem.at[g])

    weight_loads = [
        local(w_input_in, w_input_ref, load_sem.at[groups]),
        local(w_branch_in, w_branch_ref, load_sem.at[groups + 1]),
    ]
    x_load(0).start()
    weight_loads[0].start()
    for g in range(1, groups):
        x_load(g).start()
    weight_loads[1].start()

    enter_all(("seq",))
    spread_gates(gate_r_ref, gates_ref, 0, width)
    spread_gates(gate_i_ref, gates_ref, width, width)
    vec_ref[0:1, :] = conv_bias_ref[...].reshape(1, width)
    vec_ref[1:2, :] = jax.nn.softplus(-decay_ref[...].reshape(1, width))
    bias_r = bias_r_ref[...].reshape(1, width)
    bias_i = bias_i_ref[...].reshape(1, width)
    keep = [1.0 - fresh_ref[s].astype(F32) for s in range(seqs)]

    def normed_store(g):
        at = block(g, group)
        return local(normed_ref.at[at], normed_out.at[at], normed_sem.at[g])

    def norm(g):
        x_load(g).wait()
        for q in range(group // CHUNK):
            at = slice(g * group + q * CHUNK, g * group + (q + 1) * CHUNK)
            x = x_ref[at, :]
            normed_ref[at, :] = (x * mean_square(x) * gain_ref[...]).astype(BF16)

    norm(0)
    weight_loads[0].wait()
    for g in range(groups):
        if g + 1 < groups:
            norm(g + 1)
        conv = dot(normed_ref[slice(g * group, (g + 1) * group), :], w_input_ref[...])
        for j in range(group // span):
            pad_ref[g * (group // span) + j, pl.ds(TILE, span), :] = conv[
                j * span : (j + 1) * span
            ]
    for g in range(groups):
        normed_store(g).start()

    for s in range(seqs):
        tail_ref[s] = pad_ref[s, pl.ds(span, TILE), :]
    tail_copy = to_one("seq", 1, tail_ref, tail_in, send_t.at[0], recv_t.at[0])
    tail_copy.start()
    weight_loads[1].wait()

    def branch(g):
        branch_ref[block(g, group), :] = dot(normed_ref[block(g, group), :], w_branch_ref[...])

    @pl.loop(0, groups // 2)
    def _(g):
        branch(g)

    stores = [
        local(source, target, store_sem.at[i])
        for i, (source, target) in enumerate(
            (
                (branch_ref, branch_out),
                (pad_ref, pad_out),
                (pre_ref, pre_out),
                (hidden_ref, hidden_out),
            )
        )
    ]
    tail_copy.wait()
    lead = jnp.zeros((TILE - taps + 1, width), F32)
    for s in range(seqs):
        initial = jnp.concatenate(
            [lead] + [conv_init_ref[k, s : s + 1, :] * keep[s] for k in range(taps - 1)], axis=0
        )
        pad_ref[s, pl.ds(0, TILE), :] = jnp.where(me == 0, initial, tail_in[s])
    stores[1].start()

    def gates(s, slot):
        for q in range(span // ROWS):
            part = pad_ref[s, pl.ds(q * ROWS, ROWS + TILE), :]
            total = vec_ref[0:1, :]
            for k in range(taps):
                first = TILE - (taps - 1) + k
                total = total + taps_ref[k : k + 1, :] * part[first : first + ROWS]
            conv_ref[slot, pl.ds(q * ROWS, ROWS), :] = total

        pre = dot(conv_ref[slot].astype(BF16), gates_ref[...])
        pre_ref[block(s, span), :width] = pre[:, :width] + bias_r
        pre_ref[block(s, span), width:] = pre[:, width:] + bias_i
        for q in range(span // ROWS):
            rows_q = slice(q * ROWS, (q + 1) * ROWS)
            conv = conv_ref[slot, pl.ds(q * ROWS, ROWS), :]
            recall = jax.nn.sigmoid(pre[rows_q, :width] + bias_r)
            gate = jax.nn.sigmoid(pre[rows_q, width:] + bias_i)
            log_a = (-RATE_SCALE * vec_ref[1:2, :]) * recall
            a = jnp.exp(log_a)
            spaced = pl.ds(pl.multiple_of(s * pitch + q * ROWS, TILE), ROWS)
            put(a_ref, spaced, a)
            put(b_ref, spaced, jnp.sqrt(one_minus_square(log_a, a)) * gate * conv)

    per = seqs // (groups - groups // 2)

    @pl.loop(0, groups - groups // 2)
    def _(i):
        branch(groups // 2 + i)
        for j in range(per):
            gates(i * per + j, j % 2)

    stores[0].start()
    stores[2].start()

    def at_time(ref, t):
        return get(ref, pl.ds(t, seqs, stride=pitch))

    def step(t, value):
        prod, state = value
        a = at_time(a_ref, t)
        return prod * a, a * state + at_time(b_ref, t)

    ones = jnp.ones((seqs, width), F32)
    prod, state = lax.fori_loop(0, span, step, (ones, jnp.zeros_like(ones)), unroll=8)
    mine_ref[0] = prod
    mine_ref[1] = state
    sums_ref[me] = mine_ref[...]
    copies = to_all("seq", mine_ref, sums_ref, send1, recv1)
    for copy in copies:
        copy.start()

    @pl.loop(0, rows // ROWS, unroll=2)
    def _(q):
        at = block(q, ROWS)
        act_ref[at, :] = gelu(branch_ref[at, :])

    for copy in copies:
        copy.wait()

    def carry_step(j, carry):
        both = sums_ref[j]
        return jnp.where(j < me, both[0] * carry + both[1], carry)

    start = jnp.concatenate([state_ref[s : s + 1, :] * keep[s] for s in range(seqs)], axis=0)
    carry = lax.fori_loop(0, devices - 1, carry_step, start)
    carry_ref[...] = carry

    def final(t, state):
        state = at_time(a_ref, t) * state + at_time(b_ref, t)
        put(hidden_ref, pl.ds(t, seqs, stride=span), state)
        return state

    last = lax.fori_loop(0, span, final, carry, unroll=8)
    stores[3].start()
    ends_ref[0:seqs, :] = jnp.where(me == devices - 1, last, 0.0)
    for s in range(seqs):
        ends_ref[(s + 1) * TILE : (s + 2) * TILE, :] = jnp.where(
            me == devices - 1, pad_ref[s, pl.ds(span, TILE), :], 0.0
        )

    @pl.loop(0, rows // ROWS, unroll=2)
    def _(q):
        at = block(q, ROWS)
        mixed_ref[at, :] = (get(hidden_ref, at) * act_ref[at, :]).astype(BF16)

    for copy in stores:
        copy.wait()
    for g in range(groups):
        normed_store(g).wait()


def backward_kernel(
    span,
    heads,
    block_part_in,
    own_in,
    low_in,
    w_out_in,
    branch_in,
    hidden_in,
    pre_in,
    pad_in,
    normed_in,
    mixed_in,
    rest_in,
    gates_in,
    carry_ref,
    sums_ref,
    taps_ref,
    vec_ref,
    block_out,
    rec_out,
    grad_branch_out,
    input_out,
    acc_ref,
    blocks_ref,
    part,
    inbox,
    out,
    send_up,
    send_down,
    recv_up,
    recv_down,
    own_ref,
    resid_low,
    w_out_ref,
    branch_ref,
    hidden_ref,
    pre_ref,
    pad_ref,
    normed_ref,
    mixed_ref,
    a_ref,
    gd_ref,
    grad_ref,
    direct_ref,
    gpad_ref,
    heads_ref,
    low_ref,
    gates_grad,
    stage_ref,
    mine_ref,
    entries_ref,
    head_ref,
    head_in,
    load_sem,
    part_sem,
    store_sem,
    stage_sem,
    send1,
    recv1,
    send_t,
    recv_t,
    gates_ref,
    grad_branch_ref,
    input_ref,
    give_sem,
):
    seqs, width = carry_ref.shape
    taps = taps_ref.shape[0]
    rows = seqs * span
    devices, me = lax.axis_size("seq"), lax.axis_index("seq")
    n, z = lax.axis_size("mp"), lax.axis_index("mp")
    chunks = rows // CHUNK
    size = GROUP * CHUNK
    held = part.shape[0] // size
    groups = chunks // GROUP
    sems = (send_up, send_down, recv_up, recv_down)
    local = pltpu.make_async_copy

    def part_load(g):
        slot = lax.rem(g, held)
        return local(block_part_in.at[block(g, size)], part.at[block(slot, size)], part_sem.at[slot])

    loads = [
        local(source, target, load_sem.at[i])
        for i, (source, target) in enumerate(
            (
                (own_in, own_ref),
                (low_in, resid_low),
                (w_out_in, w_out_ref),
                (pre_in, pre_ref),
                (branch_in, branch_ref),
                (hidden_in, hidden_ref),
                (pad_in, pad_ref),
                (mixed_in, mixed_ref),
                (normed_in, normed_ref),
                (gates_in, gates_ref),
            )
        )
    ]
    part_load(0).start()
    for copy in loads[:6]:
        copy.start(priority=1)
    for g in range(1, held):
        part_load(g).start()
    for copy in loads[6:]:
        copy.start(priority=1)
    acc_ref[...] = jnp.zeros_like(acc_ref)
    enter_all(("seq", "mp"))

    pitch = a_ref.shape[1] // seqs

    def spaced(s, q):
        return pl.ds(pl.multiple_of(s * pitch + q * ROWS, TILE), ROWS)

    def decay(at):
        recall = jax.nn.sigmoid(pre_ref[at, :width])
        log_a = (-RATE_SCALE * vec_ref[1:2, :]) * recall
        return recall, log_a, jnp.exp(log_a)

    def piece_direct(s):
        @pl.when(s == 0)
        def _():
            for copy in loads[1:6]:
                copy.wait()

        grad_ref[...] = matmul_back(resid_low[block(s, span), :], w_out_ref[...])

        @pl.loop(0, span // ROWS)
        def _(q):
            at = block(s * (span // ROWS) + q, ROWS)
            put(a_ref, spaced(s, q), decay(at)[2])
            act, slope = gelu_both(branch_ref[at, :])
            grad = grad_ref[block(q, ROWS), :]
            put(gd_ref, spaced(s, q), grad * act)
            grad_branch_ref[at, :] = (grad * get(hidden_ref, at) * slope).astype(BF16)

    def at_time(ref, t):
        return get(ref, pl.ds(t, seqs, stride=pitch))

    zero = jnp.zeros((seqs, width), F32)
    entry_copies = to_all("seq", mine_ref, entries_ref, send1, recv1)

    def piece_entry(_):
        def step(k, through):
            t = span - 1 - k
            return at_time(a_ref, t) * (at_time(gd_ref, t) + through)

        mine_ref[...] = lax.fori_loop(0, span, step, zero, unroll=8)
        entries_ref[me] = mine_ref[...]
        for copy in entry_copies:
            copy.start()

    def piece_state(_):
        for copy in entry_copies:
            copy.wait()

        def back_step(k, through):
            j = devices - 1 - k
            return jnp.where(j > me, entries_ref[j] + sums_ref[j, 0] * through, through)

        incoming = lax.fori_loop(0, devices - 1, back_step, zero)

        def final(k, through):
            t = span - 1 - k
            grad = at_time(gd_ref, t) + through
            put(gd_ref, pl.ds(t, seqs, stride=pitch), grad)
            return at_time(a_ref, t) * grad

        lax.fori_loop(0, span, final, incoming, unroll=8)

    def add(k, value):
        acc_ref[k] += fold(value)

    parts = 2

    def piece_gates(i):
        s = i // parts
        quarters = span // ROWS // parts

        @pl.when(i == 0)
        def _():
            loads[6].wait()
            loads[9].wait()

        @pl.loop(lax.rem(i, parts) * quarters, (lax.rem(i, parts) + 1) * quarters)
        def _(q):
            at = block(s * (span // ROWS) + q, ROWS)
            part_rows = pad_ref[s, pl.ds(pl.multiple_of(q * ROWS, ROWS), ROWS + TILE), :]
            conv = vec_ref[0:1, :]
            for k in range(taps):
                first = TILE - (taps - 1) + k
                conv = conv + taps_ref[k : k + 1, :] * part_rows[first : first + ROWS]
            heads_ref[at, :] = conv.astype(BF16)
            recall, log_a, a = decay(at)
            gate = jax.nn.sigmoid(pre_ref[at, width:])
            square = one_minus_square(log_a, a)
            inverse = lax.rsqrt(square)
            root = jnp.sqrt(square)
            grad = get(gd_ref, spaced(s, q))
            hidden = get(hidden_ref, at)
            before_at = pl.multiple_of(jnp.maximum(s * span + q * ROWS - TILE, 0), TILE)
            earlier = get(hidden_ref, pl.ds(before_at, TILE))
            first_row = jnp.where(q == 0, carry_ref[pl.ds(s, 1), :], earlier[TILE - 1 :])
            place = lax.broadcasted_iota(jnp.int32, (ROWS, width), 0)
            prev = jnp.where(place == 0, first_row, pltpu.roll(hidden, 1, 0))
            grad_log = grad * a * (prev - gate * conv * a * inverse)
            through = grad_log * recall
            pre_r = through * (1.0 - recall) * (-RATE_SCALE * vec_ref[1:2, :])
            direct = grad * root * gate
            pre_i = direct * conv * (1.0 - gate)
            low_ref[at, :width] = pre_r.astype(BF16)
            low_ref[at, width:] = pre_i.astype(BF16)
            direct_ref[block(q, ROWS), :] = direct
            add(0, through)
            add(1, pre_r)
            add(2, pre_i)

        @pl.when(lax.rem(i, parts) == parts - 1)
        def _():
            whole = direct_ref[...] + matmul_back(low_ref[block(s, span), :], gates_ref[...])
            gpad_ref[s, pl.ds(0, span), :] = whole
            head_ref[s] = whole[:TILE]

    head_copy = to_one("seq", -1, head_ref, head_in, send_t.at[0], recv_t.at[0])

    def piece_head(_):
        head_copy.start()

    def piece_taps(i):
        for j in range(2):
            taps_of(2 * i + j)

    def taps_of(s):
        @pl.loop(0, span // ROWS)
        def _(q):
            at = pl.multiple_of(q * ROWS, ROWS)
            part_rows = pad_ref[s, pl.ds(at, ROWS + TILE), :]
            grad = gpad_ref[s, pl.ds(at, ROWS), :]
            add(3, grad)
            for k in range(taps):
                first = TILE - (taps - 1) + k
                add(4 + k, grad * part_rows[first : first + ROWS])

    def piece_tail(_):
        head_copy.wait()
        for s in range(seqs):
            gpad_ref[s, pl.ds(span, TILE), :] = jnp.where(me == devices - 1, 0.0, head_in[s])

    def piece_input(i):
        for j in range(2):
            input_of(2 * i + j)

    def input_of(s):
        @pl.loop(0, span // ROWS)
        def _(q):
            part_rows = gpad_ref[s, pl.ds(pl.multiple_of(q * ROWS, ROWS), ROWS + TILE), :]
            total = taps_ref[taps - 1 : taps, :] * part_rows[0:ROWS]
            for k in range(taps - 1):
                first = taps - 1 - k
                total = total + taps_ref[k : k + 1, :] * part_rows[first : first + ROWS]
            input_ref[block(s * (span // ROWS) + q, ROWS), :] = total.astype(BF16)

    def contract(left, right):
        return lax.dot_general(left, right, CONTRACT_ROWS, preferred_element_type=F32)

    head = blocks_ref.shape[0]

    gives = [
        local(grad_branch_ref, grad_branch_out, give_sem.at[0]),
        local(input_ref, input_out, give_sem.at[1]),
    ]

    def piece_give(_):
        for copy in gives:
            copy.start(priority=1)

    def piece_gates_grad(i):
        @pl.when(i == 0)
        def _():
            gates_grad[...] = contract(heads_ref[...], low_ref[:, :width])

        @pl.when(i == 1)
        def _():
            gates_grad[...] = contract(heads_ref[...], low_ref[:, width:])

        place = lax.broadcasted_iota(jnp.int32, (head, width), 1)
        line = jnp.zeros((head, width), F32)
        for h in range(heads):
            row = gates_grad[h * head : (h + 1) * head, :]
            inside = jnp.logical_and(place >= h * head, place < (h + 1) * head)
            line = jnp.where(inside, row, line)

        for j in range(2):

            @pl.when(i == j)
            def _():
                blocks_ref[:, j * width : (j + 1) * width] = line

    tall = resid_low.shape[1] // WEIGHT_STEPS

    def stage_store(i):
        at = block(lax.rem(i, WEIGHT_STEPS), tall)
        slot = lax.rem(i, 2)
        return local(
            stage_ref.at[slot],
            rec_out.at[i // WEIGHT_STEPS, at, pl.ds(0, width)],
            stage_sem.at[slot],
        )

    def piece_weights(i):
        @pl.when(i == 0)
        def _():
            loads[7].wait()
            loads[8].wait()

        @pl.loop(2 * i, 2 * i + 2)
        def _(j):
            weight_of(j)

    def weight_of(i):
        @pl.when(i >= 2)
        def _():
            stage_store(i - 2).wait()

        at = block(lax.rem(i, WEIGHT_STEPS), tall)
        slot = lax.rem(i, 2)
        for which, (left, right) in enumerate(
            ((resid_low, mixed_ref), (normed_ref, grad_branch_ref), (normed_ref, input_ref))
        ):
            @pl.when(i // WEIGHT_STEPS == which)
            def _():
                stage_ref[slot] = contract(left[:, at], right[...])

        stage_store(i).start(priority=1)

    weights = 3 * WEIGHT_STEPS
    plan = []
    begin = 3
    early = WEIGHT_STEPS // 2

    def piece_weights_later(i):
        piece_weights(i + early)

    for work, times, gap in (
        (piece_direct, seqs, 0),
        (piece_entry, 1, 0),
        (piece_weights, early, 5),
        (piece_state, 1, 0),
        (piece_gates, parts * seqs, 0),
        (piece_head, 1, 0),
        (piece_taps, seqs // 2, 0),
        (piece_gates_grad, 2, 3),
        (piece_tail, 1, 0),
        (piece_input, seqs // 2, 0),
        (piece_give, 1, 0),
        (piece_weights_later, weights // 2 - early, 0),
    ):
        plan.append((work, begin, times))
        begin += times + gap

    def run(step):
        for work, first, times in plan:
            @pl.when(jnp.logical_and(step >= first, step < first + times))
            def _():
                work(step - first)

    def before(k):
        @pl.when(k == SKEW * (n // 2))
        def _():
            loads[0].wait()

        @pl.when(jnp.logical_and(lax.rem(k, GROUP) == 0, k < chunks))
        def _():
            part_load(k // GROUP).wait()

        g = (k - out.shape[0]) // GROUP - 1 + held

        @pl.when(
            jnp.logical_and(
                jnp.logical_and(k >= out.shape[0] + GROUP, lax.rem(k - out.shape[0], GROUP) == 0),
                g < groups,
            )
        )
        def _():
            part_load(g).start(priority=1)

        run(k)

    def root(c, slot, total):
        out[slot] = own_ref[block(c // 2, CHUNK), :] + total

    def store(c, slot):
        return local(out.at[slot], block_out.at[block(c, CHUNK)], store_sem.at[slot])

    def arrive(c, slot):
        store(c, slot).start(priority=1)

    def leave(c, slot):
        store(c, slot).wait()

    line_sum(
        "mp", chunks, held * GROUP, part, inbox, out, sems, before, root, arrive, leave
    )

    @pl.loop(chunks + out.shape[0], max(begin, chunks + out.shape[0]))
    def _(k):
        run(k)

    for copy in gives:
        copy.wait()
    stage_store(weights - 2).wait()
    stage_store(weights - 1).wait()


def backward_call(span, heads, head, *args):
    block_part = args[0]
    low, w_out, branch, hidden, pre, padded, normed, mixed, rest, gates = args[2:12]
    carry, sums, taps = args[12:15]
    rows, model = block_part.shape
    seqs, width = carry.shape
    devices = lax.axis_size("seq")
    ring = ring_size("mp")
    held = 3 * GROUP * CHUNK
    dma = pltpu.SemaphoreType.DMA
    columns = pltpu.VMEM((width // LANES, seqs * (span + TILE), LANES), F32)
    return pl.pallas_call(
        functools.partial(backward_kernel, span, heads),
        out_shape=(
            shape((rows, model)),
            shape(rest.shape),
            shape((rows, width), BF16),
            shape((rows, width), BF16),
            shape((4 + taps.shape[0], TILE, width)),
            shape((head, 2 * width)),
        ),
        in_specs=[HBM] * 12 + [VMEM] * 4,
        input_output_aliases={10: 1},
        out_specs=(HBM,) * 4 + (VMEM,) * 2,
        scratch_shapes=line_scratch("mp", held, model)
        + [
            pltpu.VMEM((rows // 2, model), F32),
            pltpu.VMEM((rows, model), BF16),
            pltpu.VMEM((width, model), BF16),
            pltpu.VMEM((rows, width), F32),
            pltpu.VMEM(hidden.shape, F32),
            pltpu.VMEM(pre.shape, F32),
            pltpu.VMEM(padded.shape, F32),
            pltpu.VMEM((rows, model), BF16),
            pltpu.VMEM((rows, width), BF16),
            columns,
            columns,
            pltpu.VMEM((span, width), F32),
            pltpu.VMEM((span, width), F32),
            pltpu.VMEM((seqs, span + TILE, width), F32),
            pltpu.VMEM((rows, width), BF16),
            pltpu.VMEM((rows, 2 * width), BF16),
            pltpu.VMEM((width, width), F32),
            pltpu.VMEM((2, model // WEIGHT_STEPS, width), F32),
            pltpu.VMEM((seqs, width), F32),
            pltpu.VMEM((devices, seqs, width), F32),
            pltpu.VMEM((seqs, TILE, width), F32),
            pltpu.VMEM((seqs, TILE, width), F32),
            dma((10,)),
            dma((3,)),
            dma((ring,)),
            dma((2,)),
            dma((devices - 1,)),
            dma((devices - 1,)),
            dma((1,)),
            dma((1,)),
            pltpu.VMEM(gates.shape, BF16),
            pltpu.VMEM((rows, width), BF16),
            pltpu.VMEM((rows, width), BF16),
            dma((2,)),
        ],
        compiler_params=params(1, 63),
        cost_estimate=cost(200),
        name="backward",
    )(*args)


def line_sum(axis, total, period, part, inbox, out, sems, before, root, arrive, leave):
    send_up, send_down, recv_up, recv_down = sems
    parts = send_up.shape[0]
    columns = out.shape[2] // parts
    n, z = lax.axis_size(axis), lax.axis_index(axis)
    depth = n // 2
    ring = out.shape[0]

    def cols(p):
        return pl.ds(p * columns, columns)

    def root_of(c):
        return depth - 1 + lax.rem(c, 2)

    def up(c, step, side, p):
        slot = lax.rem(c, ring)
        return pltpu.make_async_remote_copy(
            src_ref=part.at[block(lax.rem(c, period), CHUNK), cols(p)],
            dst_ref=inbox.at[side, slot, :, cols(p)],
            send_sem=send_up.at[p, slot],
            recv_sem=recv_up.at[p, side, slot],
            device_id={axis: z + step},
            device_id_type=MESH,
        )

    def down(c, step, side, p):
        slot = lax.rem(c, ring)
        return pltpu.make_async_remote_copy(
            src_ref=out.at[slot, :, cols(p)],
            dst_ref=out.at[slot, :, cols(p)],
            send_sem=send_down.at[p, side, slot],
            recv_sem=recv_down.at[p, slot],
            device_id={axis: z + step},
            device_id_type=MESH,
        )

    inner = jnp.logical_and(z > 0, z < n - 1)

    @pl.loop(0, total + ring)
    def _(k):
        @pl.when(k >= ring)
        def _():
            c = k - ring
            r = root_of(c)
            step = jnp.where(z < r, 1, -1)
            side = jnp.where(z < r, 0, 1)

            @pl.when(z == r)
            def _():
                for p in range(parts):
                    down(c, -1, 0, p).wait_send()
                    down(c, 1, 1, p).wait_send()

            @pl.when(z != r)
            def _():
                for p in range(parts):
                    up(c, step, side, p).wait_send()

            @pl.when(jnp.logical_and(z != r, inner))
            def _():
                for p in range(parts):
                    down(c, -step, side, p).wait_send()

            leave(c, lax.rem(c, ring))

        before(k)

        for i in reversed(range(n + 1)):
            c = k - SKEW * i
            valid = jnp.logical_and(c >= 0, c < total)
            c = jnp.clip(c, 0, total - 1)
            at = block(lax.rem(c, period), CHUNK)
            slot = lax.rem(c, ring)
            r = root_of(c)
            step = jnp.where(z < r, 1, -1)
            side = jnp.where(z < r, 0, 1)
            if i > depth:
                here = jnp.logical_and(z != r, jnp.abs(z - r) == i - depth)

                @pl.when(jnp.logical_and(valid, here))
                def _():
                    for p in range(parts):
                        down(c, step, side, p).wait_recv()

                        @pl.when(inner)
                        def _():
                            down(c, -step, side, p).start()

                    arrive(c, slot)
            elif i == depth:

                @pl.when(jnp.logical_and(valid, z == r))
                def _():
                    for p in range(parts):
                        up(c, 1, 0, p).wait_recv()
                        up(c, -1, 1, p).wait_recv()
                    root(c, slot, part[at, :] + inbox[0, slot] + inbox[1, slot])
                    for p in range(parts):
                        down(c, -1, 0, p).start()
                        down(c, 1, 1, p).start()
                    arrive(c, slot)
            else:
                here = jnp.where(z < r, z, n - 1 - z) == i

                @pl.when(jnp.logical_and(valid, jnp.logical_and(z != r, here)))
                def _():
                    for p in range(parts):
                        if i > 0:
                            up(c, step, side, p).wait_recv()
                            part[at, cols(p)] += inbox[side, slot, :, cols(p)]
                        up(c, step, side, p).start()


def ring_size(axis):
    return SKEW * lax.axis_size(axis) + 4


def line_scratch(axis, rows, model, parts=2):
    dma = pltpu.SemaphoreType.DMA
    ring = ring_size(axis)
    return [
        pltpu.VMEM((rows, model), F32),
        pltpu.VMEM((2, ring, CHUNK, model), F32),
        pltpu.VMEM((ring, CHUNK, model), F32),
        dma((parts, ring)),
        dma((parts, 2, ring)),
        dma((parts, 2, ring)),
        dma((parts, ring)),
    ]


def mean_square(x):
    return lax.rsqrt(jnp.mean(x * x, axis=-1, keepdims=True) + EPS)


def nothing(*_):
    pass


def fold(value):
    total = value[0:TILE]
    for i in range(1, value.shape[0] // TILE):
        total = total + value[i * TILE : (i + 1) * TILE]
    return total


def norm_grad(value, gain, grad, acc_ref):
    q = mean_square(value)
    e = gain * grad
    acc_ref[...] += fold(grad * value * q)
    return q * e - value * (q * q * q) * jnp.mean(e * value, axis=-1, keepdims=True)


def middle_kernel(
    mixed_in,
    w_out_in,
    x_in,
    og_in,
    gain_ref,
    w_gate_in,
    w_up_in,
    w_down_in,
    normed_out,
    hidden_out,
    gate_out,
    up_out,
    glow_out,
    block_out,
    low_out,
    own_grad_out,
    weight_out,
    rest_out,
    own_out,
    acc_ref,
    part,
    inbox,
    out,
    send_up,
    send_down,
    recv_up,
    recv_down,
    mixed,
    w_out,
    w_gate,
    w_up,
    w_down,
    normed,
    rows_ref,
    og_ref,
    glow,
    gate_val,
    up_val,
    grad_hidden,
    hidden,
    grad_gate,
    grad_up,
    block_part,
    low,
    weight_sem,
    row_sem,
    og_sem,
    act_sem,
    low_sem,
    own_sem,
    again_sem,
    stage_sem,
    rest_sem,
    own_ref,
):
    n, z = lax.axis_size("mp"), lax.axis_index("mp")
    count = part.shape[0] // CHUNK
    size = GROUP * CHUNK
    groups = count // GROUP
    ring = out.shape[0]
    sems = (send_up, send_down, recv_up, recv_down)
    local = pltpu.make_async_copy

    loads = [
        local(source, target, weight_sem.at[i])
        for i, (source, target) in enumerate(
            (
                (mixed_in, mixed),
                (w_out_in, w_out),
                (w_gate_in, w_gate),
                (w_up_in, w_up),
                (w_down_in, w_down.at[slice(0, w_down_in.shape[0])]),
            )
        )
    ]
    for copy in loads:
        copy.start(priority=1)
    deep = w_down_in.shape[0]

    def og_load(g):
        return local(og_in.at[block(g, size)], og_ref, og_sem.at[0])

    og_load(0).start(priority=1)
    enter_all(("mp",))
    acc_ref[...] = jnp.zeros_like(acc_ref)
    loads[0].wait()
    loads[1].wait()

    def is_root(c):
        return z == n // 2 - 1 + lax.rem(c, 2)

    def row_load(source, c):
        slot = lax.rem(c, ring)
        at = block(lax.rem(c, count), CHUNK)
        return local(source.at[at], rows_ref.at[slot], row_sem.at[slot])

    acts = (
        (normed, normed_out),
        (glow, glow_out),
        (hidden, hidden_out),
        (grad_gate, gate_out),
        (grad_up, up_out),
        (block_part, block_out),
    )

    def act_store(i, g):
        source, target = acts[i]
        source = source.at[lax.rem(g, 2)] if i == 0 else source
        return local(source, target.at[block(g, size)], act_sem.at[i])

    def at_tick(k, first, work):
        g = (k - first) // GROUP

        @pl.when(
            jnp.logical_and(
                jnp.logical_and(k >= first, k < first + GROUP * groups),
                lax.rem(k - first, GROUP) == 0,
            )
        )
        def _():
            work(g)

    def project(g):
        def work(cols):
            part[block(g, size), cols] = dot(mixed[block(g, size), :], w_out[:, cols])

        work(slice(None))

    def piece_gate(g):
        @pl.when(g == 0)
        def _():
            for copy in loads[2:]:
                copy.wait()

        def work(cols):
            gate_val[:, cols] = dot(normed[lax.rem(g, 2)], w_gate[:, cols])

        work(slice(None))
        act_store(0, g).start(priority=1)

    def piece_up(g):
        def work(cols):
            up_val[:, cols] = dot(normed[lax.rem(g, 2)], w_up[:, cols])

        work(slice(None))

        @pl.when(g > 0)
        def _():
            for i in range(1, 6):
                act_store(i, g - 1).wait()

    def piece_low(g):
        og_load(g).wait()

        @pl.loop(0, size // ROWS)
        def _(q):
            glow[block(q, ROWS), :] = og_ref[block(q, ROWS), :].astype(BF16)

        @pl.when(g + 1 < groups)
        def _():
            og_load(g + 1).start(priority=1)

        act_store(1, g).start(priority=1)
        act_store(0, g).wait()

    def piece_hidden(g):
        def work(cols):
            grad_hidden[...] = matmul_back(glow[...], w_down[:deep, :])

        work(slice(None))

    def piece_act(g):
        @pl.loop(0, size // CHUNK)
        def _(q):
            at = block(q, CHUNK)
            up = up_val[at, :]
            grad = grad_hidden[at, :]
            act, slope = gelu_both(gate_val[at, :])
            hidden[at, :] = (act * up).astype(BF16)
            grad_gate[at, :] = (grad * up * slope).astype(BF16)
            grad_up[at, :] = (grad * act).astype(BF16)

        for i in range(2, 5):
            act_store(i, g).start(priority=1)

    def piece_down(g):
        def work(cols):
            block_part[:, cols] = dot(hidden[...], w_down[:deep, cols])

        work(slice(None))
        act_store(5, g).start(priority=1)

    def piece_back_gate(g):
        def work(cols):
            part[block(g, size), cols] = matmul_back(grad_gate[...], w_gate[cols, :])

        work(slice(None))

    def piece_back_up(g):
        def work(cols):
            part[block(g, size), cols] += matmul_back(grad_up[...], w_up[cols, :])

        work(slice(None))

    tokens = count * CHUNK
    half = tokens // 2
    quarter = half // 2
    again = [
        local(source, target, again_sem.at[i])
        for i, (source, target) in enumerate(
            (
                (normed_out, w_down.at[slice(0, tokens)]),
                (gate_out, w_gate.at[slice(0, tokens)]),
                (up_out, w_up.at[slice(0, tokens)]),
                (hidden_out, w_gate.at[slice(tokens, 2 * tokens)]),
                (glow_out.at[slice(0, half)], w_down.at[slice(tokens, tokens + half)]),
                (glow_out.at[slice(half, half + quarter)], normed.at[0]),
                (glow_out.at[slice(half + quarter, tokens)], normed.at[1]),
            )
        )
    ]
    tall = w_gate.shape[0] // WEIGHT_STEPS
    stages = (gate_val, up_val, grad_hidden)

    kept = weight_out.shape[2]
    before_rest = rest_out.shape[2] - (deep - kept)

    def stage_stores(which, i):
        at = block(i, tall)
        return (
            local(
                stages[which].at[:, pl.ds(0, kept)],
                weight_out.at[which, at],
                stage_sem.at[which],
            ),
            local(
                stages[which].at[:, pl.ds(kept, deep - kept)],
                rest_out.at[which, at, pl.ds(before_rest, deep - kept)],
                rest_sem.at[which],
            ),
        )

    own_copy = local(own_ref, own_out, rest_sem.at[3])

    def piece_reload():
        own_copy.start(priority=1)
        for i in range(1, 6):
            act_store(i, groups - 1).wait()
        for copy in again:
            copy.start(priority=1)

    def piece_ready():
        for copy in again:
            copy.wait()

    def contract(left, right):
        return lax.dot_general(left, right, CONTRACT_ROWS, preferred_element_type=F32)

    def piece_weight(step):
        i = step // 3
        at = block(i, tall)
        for which in range(3):

            @pl.when(lax.rem(step, 3) == which)
            def _():
                @pl.when(i > 0)
                def _():
                    for copy in stage_stores(which, i - 1):
                        copy.wait()

                stage = stages[which]

                def work(cols):
                    if which == 0:
                        stage[:, cols] = contract(w_down[:tokens, at], w_gate[:tokens, cols])
                    elif which == 1:
                        stage[:, cols] = contract(w_down[:tokens, at], w_up[:tokens, cols])
                    else:
                        middle = tokens + half + quarter
                        stage[:, cols] = (
                            contract(
                                w_down[tokens : tokens + half, at],
                                w_gate[tokens : tokens + half, cols],
                            )
                            + contract(normed[0, :, at], w_gate[tokens + half : middle, cols])
                            + contract(normed[1, :, at], w_gate[middle : 2 * tokens, cols])
                        )

                work(slice(None))
                for copy in stage_stores(which, i):
                    copy.start(priority=1)

    first = GROUP + SKEW * n
    spare = GROUP * groups + ring + 3
    first_weight = spare + 3
    weights = 3 * WEIGHT_STEPS

    def before(k):
        @pl.when(k == spare)
        def _():
            piece_reload()

        @pl.when(k == first_weight - 1)
        def _():
            piece_ready()

        @pl.when(jnp.logical_and(k >= first_weight, k < first_weight + weights))
        def _():
            piece_weight(k - first_weight)

        @pl.when(jnp.logical_and(k < count, is_root(k)))
        def _():
            row_load(x_in, k).start(priority=1)

        @pl.when(
            jnp.logical_and(jnp.logical_and(k >= count, k < 2 * count), is_root(k))
        )
        def _():
            row_load(og_in, k).start(priority=1)

        at_tick(k, 0, project)
        at_tick(k, first, piece_gate)
        at_tick(k, first + 1, piece_up)
        at_tick(k, first + 2, piece_low)
        at_tick(k, first + 3, piece_hidden)
        at_tick(k, first + 4, piece_act)
        at_tick(k, first + 6, piece_down)
        at_tick(k, GROUP + ring, piece_back_gate)
        at_tick(k, GROUP + ring + 2, piece_back_up)

    def root(c, slot, total):
        j = lax.rem(c, count)
        mine = block(j // 2, CHUNK)
        row_load(x_in, c).wait()

        @pl.when(c < count)
        def _():
            value = rows_ref[slot] + total
            own_ref[mine, :] = value
            out[slot] = (value * mean_square(value) * gain_ref[...]).astype(BF16).astype(F32)

        @pl.when(c >= count)
        def _():
            back = norm_grad(own_ref[mine, :], gain_ref[...], total, acc_ref)
            out[slot] = rows_ref[slot] + back

    def low_store(c, slot):
        at = block(lax.rem(c, count), CHUNK)
        return local(low.at[slot], low_out.at[at], low_sem.at[slot])

    def own_store(c, slot):
        at = block(lax.rem(c, count) // 2, CHUNK)
        return local(out.at[slot], own_grad_out.at[at], own_sem.at[slot])

    def arrive(c, slot):
        @pl.when(c < count)
        def _():
            normed[lax.rem(c // GROUP, 2), block(lax.rem(c, GROUP), CHUNK), :] = out[slot].astype(BF16)

        @pl.when(c >= count)
        def _():
            low[slot] = out[slot].astype(BF16)
            low_store(c, slot).start(priority=1)

            @pl.when(is_root(c))
            def _():
                own_store(c, slot).start(priority=1)

    def leave(c, slot):
        @pl.when(c >= count)
        def _():
            low_store(c, slot).wait()

            @pl.when(is_root(c))
            def _():
                own_store(c, slot).wait()

    line_sum("mp", 2 * count, count, part, inbox, out, sems, before, root, arrive, leave)

    own_copy.wait()
    for which in range(3):
        for copy in stage_stores(which, WEIGHT_STEPS - 1):
            copy.wait()


def middle_call(*args):
    mixed, w_out, x, og, gain, w_gate, w_up, w_down = args
    rows, model = x.shape
    width, hidden = mixed.shape[1], w_gate.shape[1]
    size = GROUP * CHUNK
    dma = pltpu.SemaphoreType.DMA
    ring = ring_size("mp")
    act = shape((rows, hidden), BF16)
    tall = shape((rows, model), BF16)
    return pl.pallas_call(
        middle_kernel,
        out_shape=(
            tall,
            act,
            act,
            act,
            tall,
            shape((rows, model)),
            tall,
            shape((rows // 2, model)),
            shape((3, model, hidden - hidden // LATER)),
            shape((3, model, width + hidden // LATER)),
            shape((rows // 2, model)),
            shape((TILE, model)),
        ),
        in_specs=[HBM] * 4 + [VMEM] + [HBM] * 3,
        out_specs=(HBM,) * 11 + (VMEM,),
        scratch_shapes=line_scratch("mp", rows, model)
        + [
            pltpu.VMEM((rows, width), BF16),
            pltpu.VMEM((width, model), BF16),
            pltpu.VMEM((model, hidden), BF16),
            pltpu.VMEM((model, hidden), BF16),
            pltpu.VMEM((max(hidden, rows * 3 // 2), model), BF16),
            pltpu.VMEM((2, size, model), BF16),
            pltpu.VMEM((ring, CHUNK, model), F32),
            pltpu.VMEM((size, model), F32),
            pltpu.VMEM((size, model), BF16),
            pltpu.VMEM((size, hidden), F32),
            pltpu.VMEM((size, hidden), F32),
            pltpu.VMEM((size, hidden), F32),
            pltpu.VMEM((size, hidden), BF16),
            pltpu.VMEM((size, hidden), BF16),
            pltpu.VMEM((size, hidden), BF16),
            pltpu.VMEM((size, model), F32),
            pltpu.VMEM((ring, CHUNK, model), BF16),
            dma((5,)),
            dma((ring,)),
            dma((1,)),
            dma((6,)),
            dma((ring,)),
            dma((ring,)),
            dma((7,)),
            dma((3,)),
            dma((4,)),
            pltpu.VMEM((rows // 2, model), F32),
        ],
        compiler_params=params(2, 63),
        cost_estimate=cost(400),
        name="middle",
    )(*args)


def last_kernel(
    own_grad_in,
    x_in,
    grad_branch_in,
    input_in,
    w_branch_in,
    w_input_in,
    gain_ref,
    other_acc,
    sums_in,
    ends_in,
    blocks_in,
    grad_out,
    norm_ref,
    small_out,
    part,
    inbox,
    out,
    send_up,
    send_down,
    recv_up,
    recv_down,
    own_grad_ref,
    x_ref,
    grad_branch,
    input_low,
    w_branch,
    w_input,
    load_sem,
    store_sem,
    acc_ref,
    mine_ref,
    seq_in,
    mp_in,
    send_s,
    recv_s,
    send_m,
    recv_m,
    small,
    small_in,
    send_v,
    recv_v,
):
    count = part.shape[0] // CHUNK
    size = GROUP * CHUNK
    sems = (send_up, send_down, recv_up, recv_down)
    local = pltpu.make_async_copy

    loads = [
        local(source, target, load_sem.at[i])
        for i, (source, target) in enumerate(
            (
                (grad_branch_in, grad_branch),
                (w_branch_in, w_branch),
                (input_in, input_low),
                (w_input_in, w_input),
                (own_grad_in, own_grad_ref),
                (x_in, x_ref),
            )
        )
    ]
    for copy in loads:
        copy.start(priority=1)
    acc_ref[...] = jnp.zeros_like(acc_ref)
    norm_ref[...] = jnp.zeros_like(norm_ref)
    enter_all(("seq", "mp"))
    for copy in loads[:4]:
        copy.wait()

    kinds = sums_in.shape[0]
    me = lax.axis_index("seq")
    width = sums_in.shape[2]
    height = kinds + ends_in.shape[0]
    head = blocks_in.shape[0]
    levels = small_in.shape[0]

    def exchange(level):
        bit = 1 << level
        partner = me + bit - 2 * bit * lax.rem(me // bit, 2)
        return pltpu.make_async_remote_copy(
            src_ref=small.at[level],
            dst_ref=small_in.at[level],
            send_sem=send_v.at[level],
            recv_sem=recv_v.at[level],
            device_id={"seq": partner},
            device_id_type=MESH,
        )

    spacing = (count - 4) // (levels + 1)
    plane = lax.axis_index("mp")

    def norm_sum(i, k, first, gaps, source):
        seq_copies = to_all("seq", mine_ref.at[i, 0], seq_in.at[i], send_s.at[i], recv_s.at[i])
        mp_copies = to_all("mp", mine_ref.at[i, 1], mp_in.at[i], send_m.at[i], recv_m.at[i])

        @pl.when(k == first)
        def _():
            mine_ref[i, 0] = jnp.sum(source[...], axis=0, keepdims=True)
            seq_in[i, me] = mine_ref[i, 0]
            for copy in seq_copies:
                copy.start()

        @pl.when(k == first + gaps[0])
        def _():
            for copy in seq_copies:
                copy.wait()
            mine_ref[i, 1] = jnp.sum(seq_in[i], axis=0)
            mp_in[i, plane] = mine_ref[i, 1]
            for copy in mp_copies:
                copy.start()

        @pl.when(k == first + gaps[0] + gaps[1])
        def _():
            for copy in mp_copies:
                copy.wait()
            norm_ref[i : i + 1, :] = jnp.sum(mp_in[i], axis=0)

    settled = count + SKEW * (lax.axis_size("mp") // 2)

    def before(k):
        @pl.when(k == 2)
        def _():
            for i in range(kinds):
                small[0, i : i + 1, :] = jnp.sum(sums_in[i], axis=0, keepdims=True)
            small[0, kinds:height, :] = ends_in[...]
            small[0, height : height + head, :] = blocks_in[:, :width]
            small[0, height + head :, :] = blocks_in[:, width:]

        for level in range(levels + 1):

            @pl.when(k == 3 + level * spacing)
            def _():
                if level > 0:
                    exchange(level - 1).wait()
                    total = small[level - 1] + small_in[level - 1]
                    if level < levels:
                        small[level] = total
                    else:
                        small_out[...] = total
                if level < levels:
                    exchange(level).start()

        norm_sum(0, k, settled, (2, 3), acc_ref)
        norm_sum(1, k, 10, (20, 20), other_acc)

        @pl.when(jnp.logical_and(lax.rem(k, 4) == 0, k // 4 < count // GROUP))
        def _():
            at = block(k // 4, size)

            def work(cols):
                part[at, cols] = matmul_back(grad_branch[at, :], w_branch[cols, :]) + matmul_back(
                    input_low[at, :], w_input[cols, :]
                )

            work(slice(None))

        @pl.when(k == SKEW * (lax.axis_size("mp") // 2))
        def _():
            for copy in loads[4:]:
                copy.wait()

    def root(c, slot, total):
        back = norm_grad(x_ref[block(c, CHUNK), :], gain_ref[...], total, acc_ref)
        out[slot] = own_grad_ref[block(c // 2, CHUNK), :] + back

    def store(c, slot):
        return local(out.at[slot], grad_out.at[block(c, CHUNK)], store_sem.at[slot])

    def arrive(c, slot):
        store(c, slot).start(priority=1)

    def leave(c, slot):
        store(c, slot).wait()

    line_sum("mp", count, count, part, inbox, out, sems, before, root, arrive, leave)


def enter_all(axes):
    barrier = pltpu.get_barrier_semaphore()
    count = 0
    for axis in axes:
        size, me = lax.axis_size(axis), lax.axis_index(axis)
        for d in range(1, size):
            pl.semaphore_signal(
                barrier, 1, device_id={axis: lax.rem(me + d, size)}, device_id_type=MESH
            )
        count += size - 1
    pl.semaphore_wait(barrier, count)


def cost(micros):
    return pl.CostEstimate(flops=int(micros * 1e9), bytes_accessed=1 << 20, transcendentals=0)


def nseq_levels():
    return (lax.axis_size("seq") - 1).bit_length()


def last_call(*args):
    x, grad_branch = args[1:3]
    rows, model = x.shape
    width = grad_branch.shape[1]
    lines = args[8].shape[0] + args[9].shape[0] + 2 * args[10].shape[0]
    levels = nseq_levels()
    dma = pltpu.SemaphoreType.DMA
    nseq, nmp = lax.axis_size("seq"), lax.axis_size("mp")
    return pl.pallas_call(
        last_kernel,
        out_shape=(shape((rows, model)), shape((TILE, model)), shape((lines, width))),
        in_specs=[HBM] * 6 + [VMEM] * 5,
        out_specs=(HBM,) + (VMEM,) * 2,
        scratch_shapes=line_scratch("mp", rows, model)
        + [
            pltpu.VMEM((rows // 2, model), F32),
            pltpu.VMEM((rows, model), F32),
            pltpu.VMEM((rows, width), BF16),
            pltpu.VMEM((rows, width), BF16),
            pltpu.VMEM((model, width), BF16),
            pltpu.VMEM((model, width), BF16),
            dma((6,)),
            dma((ring_size("mp"),)),
            pltpu.VMEM((TILE, model), F32),
            pltpu.VMEM((2, 2, 1, model), F32),
            pltpu.VMEM((2, nseq, 1, model), F32),
            pltpu.VMEM((2, nmp, 1, model), F32),
            dma((2, nseq - 1)),
            dma((2, nseq - 1)),
            dma((2, nmp - 1)),
            dma((2, nmp - 1)),
            pltpu.VMEM((levels, lines, width), F32),
            pltpu.VMEM((levels, lines, width), F32),
            dma((levels,)),
            dma((levels,)),
        ],
        compiler_params=params(4, 62),
        cost_estimate=cost(200),
        name="last_sums",
    )(*args)


def finish_kernel(
    heads,
    block_in,
    grad_in,
    mlp_in,
    rec_in,
    small_hbm,
    norm_hbm,
    decay_hbm,
    block_out,
    grad_out,
    w_gate_out,
    w_up_out,
    w_branch_out,
    w_input_out,
    w_down_out,
    w_out_out,
    gate_r_out,
    gate_i_out,
    taps_out,
    conv_bias_out,
    bias_r_out,
    bias_i_out,
    decay_out,
    norm_in_out,
    norm_mlp_out,
    state_out,
    conv_out,
    tall,
    mlp,
    rec,
    small_in,
    norm_in,
    raw_ref,
    load_sem,
    store_sem,
    extra_sem,
):
    local = pltpu.make_async_copy
    width = small_in.shape[1]
    kept = mlp.shape[2]
    late = rec.shape[2] - width
    size = grad_in.shape[0] // COPIES
    extra = [
        local(source, target, extra_sem.at[i])
        for i, (source, target) in enumerate(
            ((small_hbm, small_in), (norm_hbm, norm_in), (decay_hbm, raw_ref))
        )
    ]
    for copy in extra:
        copy.start()
    jobs = [(mlp_in, mlp, None), (rec_in, rec, None)]
    for j, (source, target) in enumerate(((block_in, block_out), (grad_in, grad_out))):
        for i in range(COPIES):
            at = slice(i * size, (i + 1) * size)
            jobs.append((source.at[at], tall.at[j, at], target.at[at]))
    loads = [local(source, held, load_sem.at[i]) for i, (source, held, _) in enumerate(jobs)]
    stores = [
        local(held, target, store_sem.at[i])
        for i, (held, target) in enumerate(
            [(held, target) for _, held, target in jobs[2:]]
            + [
                (mlp.at[0], w_gate_out.at[:, pl.ds(0, kept)]),
                (mlp.at[1], w_up_out.at[:, pl.ds(0, kept)]),
                (rec.at[0, :, pl.ds(width, late)], w_gate_out.at[:, pl.ds(kept, late)]),
                (rec.at[1, :, pl.ds(width, late)], w_up_out.at[:, pl.ds(kept, late)]),
                (rec.at[1, :, pl.ds(0, width)], w_branch_out),
                (rec.at[2, :, pl.ds(0, width)], w_input_out),
            ]
        )
    ]
    for copy in loads:
        copy.start()
    for copy in extra:
        copy.wait()
    taps, seqs, edge = taps_out.shape[0], state_out.shape[0], conv_out.shape[0]
    head = gate_r_out.shape[1]
    decay = small_in[0:1, :].reshape(width) * (RATE_SCALE * jax.nn.sigmoid(-raw_ref[...]))
    decay_out[...] = decay
    bias_r_out[...] = small_in[1:2, :].reshape(width)
    bias_i_out[...] = small_in[2:3, :].reshape(width)
    conv_bias_out[...] = small_in[3:4, :].reshape(width)
    taps_out[...] = small_in[4 : 4 + taps, :]
    begin = 4 + taps
    state_out[...] = small_in[begin : begin + seqs, :]
    for s in range(seqs):
        end = begin + seqs + (s + 1) * TILE
        for k in range(edge):
            conv_out[k, s : s + 1, :] = small_in[end - edge + k : end - edge + k + 1, :]
    begin += seqs + seqs * TILE
    for i, target in enumerate((gate_r_out, gate_i_out)):
        line = small_in[begin + i * head : begin + (i + 1) * head, :]
        for h in range(heads):
            turned = line if h == 0 else pltpu.roll(line, width - h * head, 1)
            target[h] = turned[:, :head]
    norm_in_out[...] = norm_in[0:1, :].reshape(norm_in.shape[1])
    norm_mlp_out[...] = norm_in[1:2, :].reshape(norm_in.shape[1])
    loads[0].wait()
    loads[1].wait()
    for copy in stores[2 * COPIES :]:
        copy.start()
    w_down_out[:kept, :] = mlp[2].T
    w_down_out[kept:, :] = rec[2, :, width:].T
    w_out_out[...] = rec[0, :, :width].T
    for i in range(2 * COPIES):
        loads[2 + i].wait()
        stores[i].start()
    for copy in stores:
        copy.wait()


def finish_call(seqs, heads, head, edge, *args):
    _, stream_grad, mlp_grads, rec_grads, small, norms, decay = args
    rows, model = stream_grad.shape
    own, kept = mlp_grads.shape[1:]
    width = small.shape[1]
    hidden = kept + rec_grads.shape[2] - width
    taps = edge + 1
    line = shape((width,))
    tall = shape((rows, model))
    return pl.pallas_call(
        functools.partial(finish_kernel, heads),
        out_shape=(
            tall,
            tall,
            shape((own, hidden)),
            shape((own, hidden)),
            shape((own, width)),
            shape((own, width)),
            shape((hidden, own)),
            shape((width, own)),
            shape((heads, head, head)),
            shape((heads, head, head)),
            shape((taps, width)),
            line,
            line,
            line,
            line,
            shape((model,)),
            shape((model,)),
            shape((seqs, width)),
            shape((edge, seqs, width)),
        ),
        in_specs=[HBM] * 4 + [PINNED] * 3,
        out_specs=(HBM,) * 6 + (VMEM,) * 13,
        scratch_shapes=[
            pltpu.VMEM((2, rows, model), F32),
            pltpu.VMEM(mlp_grads.shape, F32),
            pltpu.VMEM(rec_grads.shape, F32),
            pltpu.VMEM(small.shape, F32),
            pltpu.VMEM(norms.shape, F32),
            pltpu.VMEM(decay.shape, F32),
            pltpu.SemaphoreType.DMA((2 + 2 * COPIES,)),
            pltpu.SemaphoreType.DMA((6 + 2 * COPIES,)),
            pltpu.SemaphoreType.DMA((3,)),
        ],
        compiler_params=pltpu.CompilerParams(vmem_limit_bytes=63 << 20),
        cost_estimate=cost(15),
        name="finish",
    )(*args)


def params(collective, megabytes=60):
    return pltpu.CompilerParams(
        collective_id=collective, has_side_effects=True, vmem_limit_bytes=megabytes << 20
    )


def shape(dims, dtype=F32):
    return jax.ShapeDtypeStruct(dims, dtype)


def recurrence_forward(span, *args):
    x, w_input = args[:2]
    rows, model = x.shape
    seqs, width = rows // span, w_input.shape[1]
    devices = lax.axis_size("seq")
    dma = pltpu.SemaphoreType.DMA
    groups = seqs // 2
    columns = (width // LANES, rows, LANES)
    spaced = (width // LANES, seqs * (span + TILE), LANES)
    padded = (seqs, span + TILE, width)
    return pl.pallas_call(
        functools.partial(forward_kernel, span),
        out_shape=(
            shape((rows, model), BF16),
            shape((rows, width)),
            shape(padded),
            shape((rows, 2 * width)),
            shape(columns),
            shape((rows, width), BF16),
            shape((seqs, width)),
            shape((devices, 2, seqs, width)),
            shape((width, 2 * width), BF16),
            shape((TILE, width)),
            shape(((seqs + 1) * TILE, width)),
        ),
        in_specs=[HBM] * 3 + [VMEM] * 8 + [pl.BlockSpec(memory_space=pltpu.SMEM)] + [VMEM] * 2,
        out_specs=(HBM,) * 5 + (VMEM,) * 6,
        scratch_shapes=[
            pltpu.VMEM((rows, model), F32),
            pltpu.VMEM((model, width), BF16),
            pltpu.VMEM((model, width), BF16),
            pltpu.VMEM((rows, model), BF16),
            pltpu.VMEM((rows, width), F32),
            pltpu.VMEM(padded, F32),
            pltpu.VMEM((rows, 2 * width), F32),
            pltpu.VMEM(columns, F32),
            pltpu.VMEM((rows, width), F32),
            pltpu.VMEM(spaced, F32),
            pltpu.VMEM(spaced, F32),
            pltpu.VMEM((2, span, width), F32),
            pltpu.VMEM((seqs, TILE, width), F32),
            pltpu.VMEM((seqs, TILE, width), F32),
            pltpu.VMEM((2, seqs, width), F32),
            dma((groups + 2,)),
            dma((4,)),
            dma((groups,)),
            dma((devices - 1,)),
            dma((devices - 1,)),
            dma((1,)),
            dma((1,)),
        ],
        compiler_params=params(0),
        cost_estimate=cost(50),
        name="recurrence_forward",
    )(*args)


def widen(array, width):
    short = width - array.shape[-1]
    if short == 0:
        return array
    return jnp.pad(array, [(0, 0)] * (array.ndim - 1) + [(0, short)])


def per_device(
    stream,
    norm_in,
    w_branch,
    w_input,
    conv_kernel,
    conv_bias,
    gate_r,
    bias_r,
    gate_i,
    bias_i,
    decay_param,
    w_out,
    norm_mlp,
    w_gate,
    w_up,
    w_down,
    state_init,
    conv_init,
    fresh_rows,
    out_grad,
):
    seqs, span, model = stream.shape
    channels = w_branch.shape[1]
    mlp_dev = w_gate.shape[1]
    heads, head_width = gate_r.shape[:2]
    taps = conv_kernel.shape[0]
    edge = taps - 1
    rows = seqs * span
    devices = lax.axis_size("seq")
    position = lax.axis_index("seq")
    width = -(-channels // 128) * 128

    flat_in = stream.reshape(rows, model)
    flat_grad = out_grad.reshape(rows, model)
    w_branch_p = widen(w_branch, width)
    w_input_p = widen(w_input, width)
    w_out_p = jnp.pad(w_out, ((0, width - channels), (0, 0))) if width > channels else w_out
    taps_p = widen(conv_kernel, width)
    def line(value):
        return widen(value, width)

    (
        normed,
        branch,
        padded,
        pre,
        hidden,
        mixed,
        carry,
        sums,
        gates,
        rates,
        ends,
    ) = recurrence_forward(
        span,
        flat_in,
        w_input_p,
        w_branch_p,
        norm_in[None],
        taps_p,
        line(conv_bias),
        line(decay_param),
        line(bias_r),
        line(bias_i),
        gate_r,
        gate_i,
        fresh_rows,
        widen(state_init, width),
        widen(jnp.swapaxes(conv_init, 0, 1), width),
    )
    made = middle_call(mixed, w_out_p, flat_in, flat_grad, norm_mlp[None], w_gate, w_up, w_down)
    block_part, resid_low, own_grad, mlp_grads, rest, own, norm_mlp_acc = made[5:]
    mlp_grads = lax.psum_scatter(mlp_grads, "seq", scatter_dimension=1, tiled=True)
    block_out, rec_grads, grad_branch, input_low, acc, blocks = backward_call(
        span,
        heads,
        head_width,
        block_part,
        own,
        resid_low,
        w_out_p,
        branch,
        hidden,
        pre,
        padded,
        normed,
        mixed,
        rest,
        gates,
        carry,
        sums,
        taps_p,
        rates,
    )

    rec_grads, grad_branch, mlp_grads = lax.optimization_barrier(
        (rec_grads, grad_branch, mlp_grads)
    )
    rec_grads = lax.psum_scatter(rec_grads, "seq", scatter_dimension=1, tiled=True)

    stream_grad, norm_grads, small = last_call(
        own_grad,
        flat_in,
        grad_branch,
        input_low,
        w_branch_p,
        w_input_p,
        norm_in[None],
        norm_mlp_acc,
        acc,
        ends,
        blocks,
    )
    (
        block_out,
        stream_grad,
        w_gate_grad,
        w_up_grad,
        w_branch_grad,
        w_input_grad,
        w_down_grad,
        w_out_grad,
        gate_r_grad,
        gate_i_grad,
        taps_grad,
        conv_bias_grad,
        bias_r_grad,
        bias_i_grad,
        decay_grad,
        norm_in_grad,
        norm_mlp_grad,
        final_state,
        final_conv,
    ) = finish_call(
        seqs,
        heads,
        head_width,
        edge,
        block_out,
        stream_grad,
        mlp_grads,
        rec_grads,
        small,
        norm_grads,
        line(decay_param),
    )
    return (
        block_out.reshape(stream.shape),
        stream_grad.reshape(stream.shape),
        norm_in_grad,
        w_branch_grad[:, :channels],
        w_input_grad[:, :channels],
        taps_grad[:, :channels],
        conv_bias_grad[:channels],
        gate_r_grad,
        bias_r_grad[:channels],
        gate_i_grad,
        bias_i_grad[:channels],
        decay_grad[:channels],
        w_out_grad[:channels],
        norm_mlp_grad,
        w_gate_grad,
        w_up_grad,
        w_down_grad,
        final_state[:, :channels],
        jnp.swapaxes(final_conv, 0, 1)[:, :, :channels],
    )


def solution(mesh):
    seq_rows = P(None, "seq", None)
    columns = P(None, "mp")
    channel = P("mp")
    return jax.shard_map(
        per_device,
        mesh=mesh,
        in_specs=(
            seq_rows,
            P(),
            columns,
            columns,
            columns,
            channel,
            P("mp", None, None),
            channel,
            P("mp", None, None),
            channel,
            channel,
            P("mp", None),
            P(),
            columns,
            columns,
            P("mp", None),
            columns,
            P(None, None, "mp"),
            P(),
            seq_rows,
        ),
        out_specs=(
            seq_rows,
            seq_rows,
            P(),
            P("seq", "mp"),
            P("seq", "mp"),
            columns,
            channel,
            P("mp", None, None),
            channel,
            P("mp", None, None),
            channel,
            channel,
            P("mp", "seq"),
            P(),
            P("seq", "mp"),
            P("seq", "mp"),
            P("mp", "seq"),
            columns,
            P(None, None, "mp"),
        ),
        check_vma=False,
    )
```

profile of v0, /device:TPU:0, one launch (start us, length us, event | category | flops | bytes accessed | tf_op | source)
XLA Modules:
  0.0 858.2 jit_solution(6879535920986405266)
XLA Ops:
  7.2 0.0 reduce-scatter.3.cloned.1.call-start
  7.2 33.9 %recurrence_forward.1 = (bf16[1024,2048]{1,0:T(8,128)(2,1)}, f32[1024,640]{1,0:T(8,128)}, f32[8,136,640]{2,1,0:T(8,128)}, f32[1024,1280]{1,0:T(8,128)}, f32[5,10...) custom-call(f32[1024,2048]{1,0:T(8,128)} %bitcast.9, ...), custom_call_target="tpu_custom_call" | custom-call | flops 49999998976 | bytes 1048576 | tf_op jit(solution)/shard_map/recurrence_forward/pallas_call | solution.py:1855
  41.2 385.0 %middle.1 = (bf16[1024,2048]{1,0:T(8,128)(2,1)}, bf16[1024,1536]{1,0:T(8,128)(2,1)}, bf16[1024,1536]{1,0:T(8,128)(2,1)}, bf16[1024,1536]{1,0:T(8,128)(2,1)}, bf1...) custom-call(bf16[1024,640]{1,0:T(8,128)(2,1)} %get-tuple-element.68., ...), custom_call_target="tpu_custom_call" | custom-call | flops 399999991808 | bytes 1048576 | tf_op jit(solution)/shard_map/middle/pallas_call | solution.py:1379
  426.2 0.0 reduce-scatter.3.cloned.1.call-update
  426.2 0.0 reduce-scatter.5.cloned.1.call-start
  426.3 201.9 %backward.1 = (f32[1024,2048]{1,0:T(8,128)}, f32[3,2048,896]{2,1,0:T(8,128)}, bf16[1024,640]{1,0:T(8,128)(2,1)}, bf16[1024,640]{1,0:T(8,128)(2,1)}, f32[8,8,640]{2,1,0:T(8,128)}, /*index=5*/f32[160,1280]{1,0:T(8,128)}) custom-call(f32[1024,2048]{1,0:T(8,128)} %get-tuple-element.69.block_part_in, ...), custom_call_target="tpu_custom_call", output_to_operand_aliasing={{1}: (10, {})} | custom-call | flops 199999995904 | bytes 1048576 | tf_op jit(solution)/shard_map/backward/pallas_call | solution.py:775
  628.1 0.0 reduce-scatter.3.cloned.1.call-done.mlp_in
  628.2 0.0 reduce-scatter.5.cloned.1.call-update
  628.2 205.7 %last_sums.1 = (f32[1024,2048]{1,0:T(8,128)}, f32[8,2048]{1,0:T(8,128)}, f32[400,640]{1,0:T(8,128)}) custom-call(f32[512,2048]{1,0:T(8,128)} %get-tuple-element.83.own_grad_in, f32[1024,2048]{1,0:T(8,128)} %bitcast.11, bf16[1024,640]{1,0:T(8,128)(2,1)} %get-tuple-element.87.grad_branch_in, bf16[1024,640]{1,0:T(8,128)(2,1)} %get-tuple-element.88.input_in, ...), custom_call_target="tpu_custom_call" | custom-call | flops 199999995904 | bytes 1048576 | tf_op jit(solution)/shard_map/last_sums/pallas_call | solution.py:1639
  833.9 0.0 reduce-scatter.5.cloned.1.call-done.rec_in
  834.0 17.4 %finish.1 = (f32[1024,2048]{1,0:T(8,128)}, f32[1024,2048]{1,0:T(8,128)}, f32[256,1536]{1,0:T(8,128)}, f32[256,1536]{1,0:T(8,128)}, f32[256,640]{1,0:T(8,128)}, /...) custom-call(f32[1024,2048]{1,0:T(8,128)} %get-tuple-element.82.block, ...), custom_call_target="tpu_custom_call" | custom-call | flops 15000000512 | bytes 1048576 | tf_op jit(solution)/shard_map/finish/pallas_call | solution.py:1793
Async XLA Ops:
  7.2 621.0 %reduce-scatter.3.cloned.1.call-start = ((), (), s32[]{:S(2)}) async-start(), calls=%async_computation.2 | async-start | bytes 35389440 | tf_op jit(solution)/shard_map/reduce_scatter | solution.py:1982
  426.2 407.8 %reduce-scatter.5.cloned.1.call-start = ((), (), s32[]{:S(2)}) async-start(), calls=%async_computation.3 | async-start | bytes 24772608 | tf_op jit(solution)/shard_map/reduce_scatter | solution.py:2008
Sparse Core Ops, SparseCore 0:
  426.3 190.9 reduce-scatter.2
  628.3 167.7 reduce-scatter.4
where the time goes:
time: 858 us
  Pallas kernels  844 us (98%)
  between operations  14.1 us (2%)
    pallas_call x1, Pallas kernels, middle_call(): pl.pallas_call(middle_kernel, out_shape=(tall, act, act, act, tall, shape...  385 us
    pallas_call x1, Pallas kernels, last_call(): pl.pallas_call(last_kernel, out_shape=(shape((rows, model)), shape((TILE,...  206 us
    pallas_call x1, Pallas kernels, backward_call(): pl.pallas_call(functools.partial(backward_kernel, span, heads), out_shape...  202 us
    pallas_call x1, Pallas kernels, recurrence_forward(): pl.pallas_call(functools.partial(forward_kernel, span), out_shape=(shape(...  33.9 us
    pallas_call x1, Pallas kernels, finish_call(): pl.pallas_call(functools.partial(finish_kernel, heads), out_shape=(tall,...  17.4 us
  transfers between devices with their start and end apart: 2, of which 0 were waited for; matrix products, arithmetic and copies ran while one was open for 0% of the time, Pallas kernels for 47%

commit v1 on v0

--- a/solution.py
+++ b/solution.py
@@ -361,6 +361,8 @@
     mixed_in,
     rest_in,
     gates_in,
+    w_branch_in,
+    w_input_in,
     carry_ref,
     sums_ref,
     taps_ref,
@@ -369,6 +371,7 @@
     rec_out,
     grad_branch_out,
     input_out,
+    first_out,
     acc_ref,
     blocks_ref,
     part,
@@ -412,6 +415,7 @@
     grad_branch_ref,
     input_ref,
     give_sem,
+    late_sem,
 ):
     seqs, width = carry_ref.shape
     taps = taps_ref.shape[0]
@@ -614,6 +618,48 @@
 
     head = blocks_ref.shape[0]
 
+    late_loads = [
+        local(source.at[slice(i * rows, (i + 1) * rows)], target, late_sem.at[2 * j + i])
+        for j, (source, targets) in enumerate(
+            (
+                (
+                    w_branch_in,
+                    (
+                        resid_low.at[:, pl.ds(0, width)],
+                        resid_low.at[:, pl.ds(width, width)],
+                    ),
+                ),
+                (w_input_in, (resid_low.at[:, pl.ds(2 * width, width)], mixed_ref)),
+            )
+        )
+        for i, target in enumerate(targets)
+    ]
+    first_copy = local(part.at[slice(size, 2 * size)], first_out, late_sem.at[4])
+
+    def piece_projections(_):
+        for copy in late_loads:
+            copy.start(priority=1)
+
+    def piece_first(i):
+        branch_rows = grad_branch_ref[:size, :]
+        input_rows = input_ref[:size, :]
+
+        @pl.when(i == 0)
+        def _():
+            for copy in late_loads:
+                copy.wait()
+
+            part[size : 2 * size, :rows] = matmul_back(
+                branch_rows, resid_low[:, :width]
+            ) + matmul_back(input_rows, resid_low[:, 2 * width : 3 * width])
+
+        @pl.when(i == 1)
+        def _():
+            part[size : 2 * size, rows:] = matmul_back(
+                branch_rows, resid_low[:, width : 2 * width]
+            ) + matmul_back(input_rows, mixed_ref[...])
+            first_copy.start(priority=1)
+
     gives = [
         local(grad_branch_ref, grad_branch_out, give_sem.at[0]),
         local(input_ref, input_out, give_sem.at[1]),
@@ -693,7 +739,8 @@
     for work, times, gap in (
         (piece_direct, seqs, 0),
         (piece_entry, 1, 0),
-        (piece_weights, early, 5),
+        (piece_weights, early, 0),
+        (piece_projections, 1, 4),
         (piece_state, 1, 0),
         (piece_gates, parts * seqs, 0),
         (piece_head, 1, 0),
@@ -702,6 +749,7 @@
         (piece_tail, 1, 0),
         (piece_input, seqs // 2, 0),
         (piece_give, 1, 0),
+        (piece_first, 2, 0),
         (piece_weights_later, weights // 2 - early, 0),
     ):
         plan.append((work, begin, times))
@@ -757,6 +805,7 @@
 
     for copy in gives:
         copy.wait()
+    first_copy.wait()
     stage_store(weights - 2).wait()
     stage_store(weights - 1).wait()
 
@@ -764,7 +813,7 @@
 def backward_call(span, heads, head, *args):
     block_part = args[0]
     low, w_out, branch, hidden, pre, padded, normed, mixed, rest, gates = args[2:12]
-    carry, sums, taps = args[12:15]
+    carry, sums, taps = args[14:17]
     rows, model = block_part.shape
     seqs, width = carry.shape
     devices = lax.axis_size("seq")
@@ -779,12 +828,13 @@
             shape(rest.shape),
             shape((rows, width), BF16),
             shape((rows, width), BF16),
+            shape((GROUP * CHUNK, model)),
             shape((4 + taps.shape[0], TILE, width)),
             shape((head, 2 * width)),
         ),
-        in_specs=[HBM] * 12 + [VMEM] * 4,
+        in_specs=[HBM] * 14 + [VMEM] * 4,
         input_output_aliases={10: 1},
-        out_specs=(HBM,) * 4 + (VMEM,) * 2,
+        out_specs=(HBM,) * 5 + (VMEM,) * 2,
         scratch_shapes=line_scratch("mp", held, model)
         + [
             pltpu.VMEM((rows // 2, model), F32),
@@ -821,6 +871,7 @@
             pltpu.VMEM((rows, width), BF16),
             pltpu.VMEM((rows, width), BF16),
             dma((2,)),
+            dma((5,)),
         ],
         compiler_params=params(1, 63),
         cost_estimate=cost(200),
@@ -1394,7 +1445,7 @@
         ),
         in_specs=[HBM] * 4 + [VMEM] + [HBM] * 3,
         out_specs=(HBM,) * 11 + (VMEM,),
-        scratch_shapes=line_scratch("mp", rows, model)
+        scratch_shapes=line_scratch("mp", rows, model, 4)
         + [
             pltpu.VMEM((rows, width), BF16),
             pltpu.VMEM((width, model), BF16),
@@ -1431,6 +1482,7 @@
 
 
 def last_kernel(
+    first_in,
     own_grad_in,
     x_in,
     grad_branch_in,
@@ -1491,13 +1543,14 @@
             )
         )
     ]
+    first_load = local(first_in, part.at[slice(0, size)], load_sem.at[6])
+    first_load.start()
     for copy in loads:
         copy.start(priority=1)
     acc_ref[...] = jnp.zeros_like(acc_ref)
     norm_ref[...] = jnp.zeros_like(norm_ref)
     enter_all(("seq", "mp"))
-    for copy in loads[:4]:
-        copy.wait()
+    first_load.wait()
 
     kinds = sums_in.shape[0]
     me = lax.axis_index("seq")
@@ -1575,7 +1628,16 @@
         norm_sum(0, k, settled, (2, 3), acc_ref)
         norm_sum(1, k, 10, (20, 20), other_acc)
 
-        @pl.when(jnp.logical_and(lax.rem(k, 4) == 0, k // 4 < count // GROUP))
+        @pl.when(k == 4)
+        def _():
+            for copy in loads[:4]:
+                copy.wait()
+
+        @pl.when(
+            jnp.logical_and(
+                lax.rem(k, 4) == 0, jnp.logical_and(k > 0, k // 4 < count // GROUP)
+            )
+        )
         def _():
             at = block(k // 4, size)
 
@@ -1629,17 +1691,17 @@
 
 
 def last_call(*args):
-    x, grad_branch = args[1:3]
+    x, grad_branch = args[2:4]
     rows, model = x.shape
     width = grad_branch.shape[1]
-    lines = args[8].shape[0] + args[9].shape[0] + 2 * args[10].shape[0]
+    lines = args[9].shape[0] + args[10].shape[0] + 2 * args[11].shape[0]
     levels = nseq_levels()
     dma = pltpu.SemaphoreType.DMA
     nseq, nmp = lax.axis_size("seq"), lax.axis_size("mp")
     return pl.pallas_call(
         last_kernel,
         out_shape=(shape((rows, model)), shape((TILE, model)), shape((lines, width))),
-        in_specs=[HBM] * 6 + [VMEM] * 5,
+        in_specs=[HBM] * 7 + [VMEM] * 5,
         out_specs=(HBM,) + (VMEM,) * 2,
         scratch_shapes=line_scratch("mp", rows, model)
         + [
@@ -1649,7 +1711,7 @@
             pltpu.VMEM((rows, width), BF16),
             pltpu.VMEM((model, width), BF16),
             pltpu.VMEM((model, width), BF16),
-            dma((6,)),
+            dma((7,)),
             dma((ring_size("mp"),)),
             pltpu.VMEM((TILE, model), F32),
             pltpu.VMEM((2, 2, 1, model), F32),
@@ -1980,7 +2042,7 @@
     made = middle_call(mixed, w_out_p, flat_in, flat_grad, norm_mlp[None], w_gate, w_up, w_down)
     block_part, resid_low, own_grad, mlp_grads, rest, own, norm_mlp_acc = made[5:]
     mlp_grads = lax.psum_scatter(mlp_grads, "seq", scatter_dimension=1, tiled=True)
-    block_out, rec_grads, grad_branch, input_low, acc, blocks = backward_call(
+    block_out, rec_grads, grad_branch, input_low, first_rows, acc, blocks = backward_call(
         span,
         heads,
         head_width,
@@ -1996,6 +2058,8 @@
         mixed,
         rest,
         gates,
+        w_branch_p,
+        w_input_p,
         carry,
         sums,
         taps_p,
@@ -2008,6 +2072,7 @@
     rec_grads = lax.psum_scatter(rec_grads, "seq", scatter_dimension=1, tiled=True)
 
     stream_grad, norm_grads, small = last_call(
+        first_rows,
         own_grad,
         flat_in,
         grad_branch,

time: 858 us -> 857 us (level)
  no operation moved by 1% of the time
where the time goes in v1:
time: 857 us
  Pallas kernels  842 us (98%)
  between operations  14.1 us (2%)
    pallas_call x1, Pallas kernels, middle_call(): pl.pallas_call(middle_kernel, out_shape=(tall, act, act, act, tall, shape...  386 us
    pallas_call x1, Pallas kernels, last_call(): pl.pallas_call(last_kernel, out_shape=(shape((rows, model)), shape((TILE,...  203 us
    pallas_call x1, Pallas kernels, backward_call(): pl.pallas_call(functools.partial(backward_kernel, span, heads), out_shape...  202 us
    pallas_call x1, Pallas kernels, recurrence_forward(): pl.pallas_call(functools.partial(forward_kernel, span), out_shape=(shape(...  34 us
    pallas_call x1, Pallas kernels, finish_call(): pl.pallas_call(functools.partial(finish_kernel, heads), out_shape=(tall,...  17.3 us
  transfers between devices with their start and end apart: 2, of which 0 were waited for; matrix products, arithmetic and copies ran while one was open for 0% of the time, Pallas kernels for 47%

profile of v1, /device:TPU:0, one launch (start us, length us, event | category | flops | bytes accessed | tf_op | source)
XLA Modules:
  0.0 856.8 jit_solution(15129191530670367344)
XLA Ops:
  7.2 0.0 reduce-scatter.3.cloned.1.call-start
  7.2 34.0 %recurrence_forward.1 = (bf16[1024,2048]{1,0:T(8,128)(2,1)}, f32[1024,640]{1,0:T(8,128)}, f32[8,136,640]{2,1,0:T(8,128)}, f32[1024,1280]{1,0:T(8,128)}, f32[5,10...) custom-call(f32[1024,2048]{1,0:T(8,128)} %bitcast.9, ...), custom_call_target="tpu_custom_call" | custom-call | flops 49999998976 | bytes 1048576 | tf_op jit(solution)/shard_map/recurrence_forward/pallas_call | solution.py:1917
  41.2 386.3 %middle.1 = (bf16[1024,2048]{1,0:T(8,128)(2,1)}, bf16[1024,1536]{1,0:T(8,128)(2,1)}, bf16[1024,1536]{1,0:T(8,128)(2,1)}, bf16[1024,1536]{1,0:T(8,128)(2,1)}, bf1...) custom-call(bf16[1024,640]{1,0:T(8,128)(2,1)} %get-tuple-element.69., ...), custom_call_target="tpu_custom_call" | custom-call | flops 399999991808 | bytes 1048576 | tf_op jit(solution)/shard_map/middle/pallas_call | solution.py:1430
  427.5 0.0 reduce-scatter.3.cloned.1.call-update
  427.5 0.0 reduce-scatter.5.cloned.1.call-start
  427.6 202.3 %backward.1 = (f32[1024,2048]{1,0:T(8,128)}, f32[3,2048,896]{2,1,0:T(8,128)}, bf16[1024,640]{1,0:T(8,128)(2,1)}, bf16[1024,640]{1,0:T(8,128)(2,1)}, f32[256,2048...) custom-call(f32[1024,2048]{1,0:T(8,128)} %get-tuple-element.70.block_part_in, ...), custom_call_target="tpu_custom_call", output_to_operand_aliasing={{1}: (10, {})} | custom-call | flops 199999995904 | bytes 1048576 | tf_op jit(solution)/shard_map/backward/pallas_call | solution.py:824
  629.9 0.0 reduce-scatter.3.cloned.1.call-done.mlp_in
  629.9 0.0 reduce-scatter.5.cloned.1.call-update
  630.0 202.6 %last_sums.1 = (f32[1024,2048]{1,0:T(8,128)}, f32[8,2048]{1,0:T(8,128)}, f32[400,640]{1,0:T(8,128)}) custom-call(f32[256,2048]{1,0:T(8,128)} %get-tuple-element.84.first_in, f32[512,2048]{1,0:T(8,128)} %get-tuple-element.85.own_grad_in, f32[1024,2048]{1,0:T(8,128)} %bitcast.11, bf16[1024,640]{1,0:T(8,128)(2,1)} %get-tuple-element.89.grad_branch_in, ...), custom_call_target="tpu_custom_call" | custom-call | flops 199999995904 | bytes 1048576 | tf_op jit(solution)/shard_map/last_sums/pallas_call | solution.py:1701
  832.6 0.0 reduce-scatter.5.cloned.1.call-done.rec_in
  832.6 17.3 %finish.1 = (f32[1024,2048]{1,0:T(8,128)}, f32[1024,2048]{1,0:T(8,128)}, f32[256,1536]{1,0:T(8,128)}, f32[256,1536]{1,0:T(8,128)}, f32[256,640]{1,0:T(8,128)}, /...) custom-call(f32[1024,2048]{1,0:T(8,128)} %get-tuple-element.83.block, ...), custom_call_target="tpu_custom_call" | custom-call | flops 15000000512 | bytes 1048576 | tf_op jit(solution)/shard_map/finish/pallas_call | solution.py:1855
Async XLA Ops:
  7.2 622.7 %reduce-scatter.3.cloned.1.call-start = ((), (), s32[]{:S(2)}) async-start(), calls=%async_computation.2 | async-start | bytes 35389440 | tf_op jit(solution)/shard_map/reduce_scatter | solution.py:2044
  427.5 405.1 %reduce-scatter.5.cloned.1.call-start = ((), (), s32[]{:S(2)}) async-start(), calls=%async_computation.3 | async-start | bytes 24772608 | tf_op jit(solution)/shard_map/reduce_scatter | solution.py:2072
Sparse Core Ops, SparseCore 0:
  427.6 191.4 reduce-scatter.2
  630.1 167.0 reduce-scatter.4

commit v2 on v1

--- a/solution.py
+++ b/solution.py
@@ -1156,10 +1156,7 @@
             work(g)
 
     def project(g):
-        def work(cols):
-            part[block(g, size), cols] = dot(mixed[block(g, size), :], w_out[:, cols])
-
-        work(slice(None))
+        part[block(g, size), :] = dot(mixed[block(g, size), :], w_out[...])
 
     def piece_gate(g):
         @pl.when(g == 0)
@@ -1353,7 +1350,14 @@
         def _():
             row_load(og_in, k).start(priority=1)
 
-        at_tick(k, 0, project)
+        @pl.when(k == 0)
+        def _():
+            project(0)
+
+        @pl.when(jnp.logical_and(lax.rem(k, GROUP) == GROUP // 2, k < (groups - 1) * GROUP))
+        def _():
+            project(k // GROUP + 1)
+
         at_tick(k, first, piece_gate)
         at_tick(k, first + 1, piece_up)
         at_tick(k, first + 2, piece_low)
@@ -1445,7 +1449,7 @@
         ),
         in_specs=[HBM] * 4 + [VMEM] + [HBM] * 3,
         out_specs=(HBM,) * 11 + (VMEM,),
-        scratch_shapes=line_scratch("mp", rows, model, 4)
+        scratch_shapes=line_scratch("mp", rows, model)
         + [
             pltpu.VMEM((rows, width), BF16),
             pltpu.VMEM((width, model), BF16),

time: 857 us -> 856 us (level)
  no operation moved by 1% of the time
where the time goes in v2:
time: 856 us
  Pallas kernels  842 us (98%)
  between operations  14.1 us (2%)
    pallas_call x1, Pallas kernels, middle_call(): pl.pallas_call(middle_kernel, out_shape=(tall, act, act, act, tall, shape...  385 us
    pallas_call x1, Pallas kernels, last_call(): pl.pallas_call(last_kernel, out_shape=(shape((rows, model)), shape((TILE,...  204 us
    pallas_call x1, Pallas kernels, backward_call(): pl.pallas_call(functools.partial(backward_kernel, span, heads), out_shape...  202 us
    pallas_call x1, Pallas kernels, recurrence_forward(): pl.pallas_call(functools.partial(forward_kernel, span), out_shape=(shape(...  34 us
    pallas_call x1, Pallas kernels, finish_call(): pl.pallas_call(functools.partial(finish_kernel, heads), out_shape=(tall,...  17.3 us
  transfers between devices with their start and end apart: 2, of which 0 were waited for; matrix products, arithmetic and copies ran while one was open for 0% of the time, Pallas kernels for 47%

profile of v2, /device:TPU:0, one launch (start us, length us, event | category | flops | bytes accessed | tf_op | source)
XLA Modules:
  0.0 855.8 jit_solution(14432314061052068201)
XLA Ops:
  7.2 0.0 reduce-scatter.3.cloned.1.call-start
  7.2 34.0 %recurrence_forward.1 = (bf16[1024,2048]{1,0:T(8,128)(2,1)}, f32[1024,640]{1,0:T(8,128)}, f32[8,136,640]{2,1,0:T(8,128)}, f32[1024,1280]{1,0:T(8,128)}, f32[5,10...) custom-call(f32[1024,2048]{1,0:T(8,128)} %bitcast.9, ...), custom_call_target="tpu_custom_call" | custom-call | flops 49999998976 | bytes 1048576 | tf_op jit(solution)/shard_map/recurrence_forward/pallas_call | solution.py:1921
  41.2 384.8 %middle.1 = (bf16[1024,2048]{1,0:T(8,128)(2,1)}, bf16[1024,1536]{1,0:T(8,128)(2,1)}, bf16[1024,1536]{1,0:T(8,128)(2,1)}, bf16[1024,1536]{1,0:T(8,128)(2,1)}, bf1...) custom-call(bf16[1024,640]{1,0:T(8,128)(2,1)} %get-tuple-element.69., ...), custom_call_target="tpu_custom_call" | custom-call | flops 399999991808 | bytes 1048576 | tf_op jit(solution)/shard_map/middle/pallas_call | solution.py:1434
  426.0 0.0 reduce-scatter.3.cloned.1.call-update
  426.1 0.0 reduce-scatter.5.cloned.1.call-start
  426.1 201.9 %backward.1 = (f32[1024,2048]{1,0:T(8,128)}, f32[3,2048,896]{2,1,0:T(8,128)}, bf16[1024,640]{1,0:T(8,128)(2,1)}, bf16[1024,640]{1,0:T(8,128)(2,1)}, f32[256,2048...) custom-call(f32[1024,2048]{1,0:T(8,128)} %get-tuple-element.70.block_part_in, ...), custom_call_target="tpu_custom_call", output_to_operand_aliasing={{1}: (10, {})} | custom-call | flops 199999995904 | bytes 1048576 | tf_op jit(solution)/shard_map/backward/pallas_call | solution.py:824
  628.1 0.0 reduce-scatter.3.cloned.1.call-done.mlp_in
  628.1 0.0 reduce-scatter.5.cloned.1.call-update
  628.1 203.5 %last_sums.1 = (f32[1024,2048]{1,0:T(8,128)}, f32[8,2048]{1,0:T(8,128)}, f32[400,640]{1,0:T(8,128)}) custom-call(f32[256,2048]{1,0:T(8,128)} %get-tuple-element.84.first_in, f32[512,2048]{1,0:T(8,128)} %get-tuple-element.85.own_grad_in, f32[1024,2048]{1,0:T(8,128)} %bitcast.11, bf16[1024,640]{1,0:T(8,128)(2,1)} %get-tuple-element.89.grad_branch_in, ...), custom_call_target="tpu_custom_call" | custom-call | flops 199999995904 | bytes 1048576 | tf_op jit(solution)/shard_map/last_sums/pallas_call | solution.py:1705
  831.6 0.0 reduce-scatter.5.cloned.1.call-done.rec_in
  831.7 17.3 %finish.1 = (f32[1024,2048]{1,0:T(8,128)}, f32[1024,2048]{1,0:T(8,128)}, f32[256,1536]{1,0:T(8,128)}, f32[256,1536]{1,0:T(8,128)}, f32[256,640]{1,0:T(8,128)}, /...) custom-call(f32[1024,2048]{1,0:T(8,128)} %get-tuple-element.83.block, ...), custom_call_target="tpu_custom_call" | custom-call | flops 15000000512 | bytes 1048576 | tf_op jit(solution)/shard_map/finish/pallas_call | solution.py:1859
Async XLA Ops:
  7.2 620.9 %reduce-scatter.3.cloned.1.call-start = ((), (), s32[]{:S(2)}) async-start(), calls=%async_computation.2 | async-start | bytes 35389440 | tf_op jit(solution)/shard_map/reduce_scatter | solution.py:2048
  426.1 405.6 %reduce-scatter.5.cloned.1.call-start = ((), (), s32[]{:S(2)}) async-start(), calls=%async_computation.3 | async-start | bytes 24772608 | tf_op jit(solution)/shard_map/reduce_scatter | solution.py:2076
Sparse Core Ops, SparseCore 0:
  426.2 190.8 reduce-scatter.2
  628.2 169.9 reduce-scatter.4

commit v3 on v2

--- a/solution.py
+++ b/solution.py
@@ -220,7 +220,7 @@
                 j * span : (j + 1) * span
             ]
     for g in range(groups):
-        normed_store(g).start()
+        normed_store(g).start(priority=1)
 
     for s in range(seqs):
         tail_ref[s] = pad_ref[s, pl.ds(span, TILE), :]
@@ -253,7 +253,7 @@
             [lead] + [conv_init_ref[k, s : s + 1, :] * keep[s] for k in range(taps - 1)], axis=0
         )
         pad_ref[s, pl.ds(0, TILE), :] = jnp.where(me == 0, initial, tail_in[s])
-    stores[1].start()
+    stores[1].start(priority=1)
 
     def gates(s, slot):
         for q in range(span // ROWS):
@@ -286,8 +286,8 @@
         for j in range(per):
             gates(i * per + j, j % 2)
 
-    stores[0].start()
-    stores[2].start()
+    stores[0].start(priority=1)
+    stores[2].start(priority=1)
 
     def at_time(ref, t):
         return get(ref, pl.ds(t, seqs, stride=pitch))
@@ -328,7 +328,7 @@
         return state
 
     last = lax.fori_loop(0, span, final, carry, unroll=8)
-    stores[3].start()
+    stores[3].start(priority=1)
     ends_ref[0:seqs, :] = jnp.where(me == devices - 1, last, 0.0)
     for s in range(seqs):
         ends_ref[(s + 1) * TILE : (s + 2) * TILE, :] = jnp.where(
@@ -1836,13 +1836,13 @@
     loads[0].wait()
     loads[1].wait()
     for copy in stores[2 * COPIES :]:
-        copy.start()
+        copy.start(priority=1)
     w_down_out[:kept, :] = mlp[2].T
     w_down_out[kept:, :] = rec[2, :, width:].T
     w_out_out[...] = rec[0, :, :width].T
     for i in range(2 * COPIES):
         loads[2 + i].wait()
-        stores[i].start()
+        stores[i].start(priority=1)
     for copy in stores:
         copy.wait()
 

time: 856 us -> 856 us (level)
  no operation moved by 1% of the time
where the time goes in v3:
time: 856 us
  Pallas kernels  842 us (98%)
  between operations  14.1 us (2%)
    pallas_call x1, Pallas kernels, middle_call(): pl.pallas_call(middle_kernel, out_shape=(tall, act, act, act, tall, shape...  385 us
    pallas_call x1, Pallas kernels, last_call(): pl.pallas_call(last_kernel, out_shape=(shape((rows, model)), shape((TILE,...  204 us
    pallas_call x1, Pallas kernels, backward_call(): pl.pallas_call(functools.partial(backward_kernel, span, heads), out_shape...  202 us
    pallas_call x1, Pallas kernels, recurrence_forward(): pl.pallas_call(functools.partial(forward_kernel, span), out_shape=(shape(...  34 us
    pallas_call x1, Pallas kernels, finish_call(): pl.pallas_call(functools.partial(finish_kernel, heads), out_shape=(tall,...  17.3 us
  transfers between devices with their start and end apart: 2, of which 0 were waited for; matrix products, arithmetic and copies ran while one was open for 0% of the time, Pallas kernels for 47%

profile of v3, /device:TPU:0, one launch (start us, length us, event | category | flops | bytes accessed | tf_op | source)
XLA Modules:
  0.0 855.8 jit_solution(4351512761236535356)
XLA Ops:
  7.2 0.0 reduce-scatter.3.cloned.1.call-start
  7.2 34.0 %recurrence_forward.1 = (bf16[1024,2048]{1,0:T(8,128)(2,1)}, f32[1024,640]{1,0:T(8,128)}, f32[8,136,640]{2,1,0:T(8,128)}, f32[1024,1280]{1,0:T(8,128)}, f32[5,10...) custom-call(f32[1024,2048]{1,0:T(8,128)} %bitcast.9, ...), custom_call_target="tpu_custom_call" | custom-call | flops 49999998976 | bytes 1048576 | tf_op jit(solution)/shard_map/recurrence_forward/pallas_call | solution.py:1921
  41.2 384.8 %middle.1 = (bf16[1024,2048]{1,0:T(8,128)(2,1)}, bf16[1024,1536]{1,0:T(8,128)(2,1)}, bf16[1024,1536]{1,0:T(8,128)(2,1)}, bf16[1024,1536]{1,0:T(8,128)(2,1)}, bf1...) custom-call(bf16[1024,640]{1,0:T(8,128)(2,1)} %get-tuple-element.69., ...), custom_call_target="tpu_custom_call" | custom-call | flops 399999991808 | bytes 1048576 | tf_op jit(solution)/shard_map/middle/pallas_call | solution.py:1434
  426.0 0.0 reduce-scatter.3.cloned.1.call-update
  426.1 0.0 reduce-scatter.5.cloned.1.call-start
  426.1 201.9 %backward.1 = (f32[1024,2048]{1,0:T(8,128)}, f32[3,2048,896]{2,1,0:T(8,128)}, bf16[1024,640]{1,0:T(8,128)(2,1)}, bf16[1024,640]{1,0:T(8,128)(2,1)}, f32[256,2048...) custom-call(f32[1024,2048]{1,0:T(8,128)} %get-tuple-element.70.block_part_in, ...), custom_call_target="tpu_custom_call", output_to_operand_aliasing={{1}: (10, {})} | custom-call | flops 199999995904 | bytes 1048576 | tf_op jit(solution)/shard_map/backward/pallas_call | solution.py:824
  628.1 0.0 reduce-scatter.3.cloned.1.call-done.mlp_in
  628.1 0.0 reduce-scatter.5.cloned.1.call-update
  628.1 203.5 %last_sums.1 = (f32[1024,2048]{1,0:T(8,128)}, f32[8,2048]{1,0:T(8,128)}, f32[400,640]{1,0:T(8,128)}) custom-call(f32[256,2048]{1,0:T(8,128)} %get-tuple-element.84.first_in, f32[512,2048]{1,0:T(8,128)} %get-tuple-element.85.own_grad_in, f32[1024,2048]{1,0:T(8,128)} %bitcast.11, bf16[1024,640]{1,0:T(8,128)(2,1)} %get-tuple-element.89.grad_branch_in, ...), custom_call_target="tpu_custom_call" | custom-call | flops 199999995904 | bytes 1048576 | tf_op jit(solution)/shard_map/last_sums/pallas_call | solution.py:1705
  831.6 0.0 reduce-scatter.5.cloned.1.call-done.rec_in
  831.7 17.3 %finish.1 = (f32[1024,2048]{1,0:T(8,128)}, f32[1024,2048]{1,0:T(8,128)}, f32[256,1536]{1,0:T(8,128)}, f32[256,1536]{1,0:T(8,128)}, f32[256,640]{1,0:T(8,128)}, /...) custom-call(f32[1024,2048]{1,0:T(8,128)} %get-tuple-element.83.block, ...), custom_call_target="tpu_custom_call" | custom-call | flops 15000000512 | bytes 1048576 | tf_op jit(solution)/shard_map/finish/pallas_call | solution.py:1859
Async XLA Ops:
  7.2 620.9 %reduce-scatter.3.cloned.1.call-start = ((), (), s32[]{:S(2)}) async-start(), calls=%async_computation.2 | async-start | bytes 35389440 | tf_op jit(solution)/shard_map/reduce_scatter | solution.py:2048
  426.1 405.6 %reduce-scatter.5.cloned.1.call-start = ((), (), s32[]{:S(2)}) async-start(), calls=%async_computation.3 | async-start | bytes 24772608 | tf_op jit(solution)/shard_map/reduce_scatter | solution.py:2076
Sparse Core Ops, SparseCore 0:
  426.2 190.8 reduce-scatter.2
  628.2 169.9 reduce-scatter.4
